TPU v7x, 128 devices: a whole 4x4x4 slice. The times are simulated.
128 devices in a mesh: lab: 8 (over z, core), leaf: 16 (over y, x).
Axes of the slice: x: 4, y: 4, z: 4, core: 2. Of those that a mesh axis runs over, the one named last changes fastest.
Arguments:
- query_tokens: int32 [4096, 32], P(('lab', 'leaf')), may hold values from 0 to 32767
- label_tokens: int32 [8192, 32], P(('lab', 'leaf')), may hold values from 0 to 32767
- label_node: int32 [8192], replicated, may hold values from 0 to 15, as said below
- shortlist_owner: int32 [4096, 8], P(('lab', 'leaf')), may hold values from 0 to 127, as said below
- shortlist_node: int32 [4096, 8, 8], P(('lab', 'leaf')), may hold values from 0 to 15, as said below
- positives: int32 [4096, 4], P(('lab', 'leaf')), may hold values from 0 to 8191, as said below
- token_lookup_table: bfloat16 [32768, 256], replicated, may hold values from -6 to 6
- width_three_filters: bfloat16 [768, 512], replicated, may hold values from -0.21875 to 0.21875
- width_five_filters: bfloat16 [1280, 512], replicated, may hold values from -0.15625 to 0.15625
- projection: bfloat16 [1024, 512], replicated, may hold values from -0.1875 to 0.1875
- free_vectors: bfloat16 [2048, 512], P(('lab', 'leaf')), may hold values from -4 to 4
Outputs:
- query_loss: float32 [4096], P(('lab', 'leaf'))
- grad_free: float32 [2048, 512], P(('lab', 'leaf'))
- grad_three: float32 [768, 512], P('leaf')
- grad_five: float32 [1280, 512], P('leaf')
- grad_projection: float32 [1024, 512], P('leaf')
Inputs may be any that keep to these rules, and one draw needn't show every extreme that they name: `label_node`: every node of a device belongs to at least one of that device's 64 labels. `shortlist_owner`: the 8 owners of one query differ. Among the 32 queries of one device at most 8 name the same owner; one owner, the same on every device, is named by exactly 8 queries of every device. `shortlist_node`: the 8 nodes listed for one query and owner differ. `positives`: each positive label belongs to a node of its query's shortlist.
All inputs are finite; a program needn't handle non-finite values.
Results may differ from a plain program's by a relative error of at most 0.0035.
Values may be sent and summed in bfloat16 or wider, within the bound.
A program may use at most 128 MiB of HBM per device.

v0:
```python
import jax
import jax.numpy as jnp
from jax import lax
from jax.sharding import PartitionSpec as P

CAP = 8


SCORE_SCALE = 0.25


def unfold(token_numbers, token_lookup_table, kernel_width):
    titles, length = token_numbers.shape
    embedded = jnp.take(token_lookup_table, token_numbers, axis=0)
    margin = kernel_width // 2
    padded = jnp.pad(embedded, ((0, 0), (margin, margin), (0, 0)))
    stacked = jnp.concatenate(
        [padded[:, offset : offset + length, :] for offset in range(kernel_width)], axis=2
    )
    return stacked.reshape(titles * length, kernel_width * token_lookup_table.shape[1])


def gelu_tanh(values):
    return jax.nn.gelu(values, approximate=True)


def encode(token_numbers, token_lookup_table, width_three_filters, width_five_filters, projection):
    titles, length = token_numbers.shape
    three_taps = unfold(token_numbers, token_lookup_table, 3)
    five_taps = unfold(token_numbers, token_lookup_table, 5)
    preact = jnp.concatenate(
        [
            jnp.dot(three_taps, width_three_filters, preferred_element_type=jnp.float32),
            jnp.dot(five_taps, width_five_filters, preferred_element_type=jnp.float32),
        ],
        axis=1,
    )
    pooled = jnp.mean(gelu_tanh(preact).reshape(titles, length, -1), axis=1).astype(jnp.bfloat16)
    encoded = jnp.dot(pooled, projection, preferred_element_type=jnp.float32)
    return (three_taps, five_taps, preact, pooled, encoded)


def backward_pass(
    three_taps, five_taps, preact, pooled, grad_encoded, projection, channels, length
):
    upstream = grad_encoded.astype(jnp.bfloat16)
    grad_projection = jnp.dot(pooled.T, upstream, preferred_element_type=jnp.float32)
    grad_pooled = jnp.dot(upstream, projection.T, preferred_element_type=jnp.float32)
    spread = jnp.repeat(grad_pooled / length, length, axis=0)
    unused_out, pullback = jax.vjp(gelu_tanh, preact)
    grad_preact = pullback(spread)[0].astype(jnp.bfloat16)
    grad_three = jnp.dot(
        three_taps.T, grad_preact[:, :channels], preferred_element_type=jnp.float32
    )
    grad_five = jnp.dot(five_taps.T, grad_preact[:, channels:], preferred_element_type=jnp.float32)
    return (grad_three, grad_five, grad_projection)


def per_device(
    query_tokens,
    label_tokens,
    label_node,
    shortlist_owner,
    shortlist_node,
    positives,
    token_lookup_table,
    width_three_filters,
    width_five_filters,
    projection,
    free_vectors,
):
    leaf_count = lax.axis_size("leaf")
    devices = lax.axis_size("lab") * leaf_count
    device_index = lax.axis_index("lab") * leaf_count + lax.axis_index("leaf")
    query_count = query_tokens.shape[0]
    label_count = label_tokens.shape[0]
    node_count = free_vectors.shape[0]
    model_width = projection.shape[1]
    owners_each = shortlist_node.shape[1]
    listed_count = shortlist_node.shape[2]
    length = query_tokens.shape[1]
    titles = jnp.concatenate([query_tokens, label_tokens], axis=0)
    three_taps, five_taps, preact, pooled, encoded = encode(
        titles, token_lookup_table, width_three_filters, width_five_filters, projection
    )
    query_rows = encoded[:query_count].astype(jnp.bfloat16)
    label_encoded = encoded[query_count:]
    own_nodes = lax.dynamic_slice_in_dim(label_node, device_index * label_count, label_count)
    node_iota = jnp.arange(node_count, dtype=jnp.int32)
    membership = (own_nodes[:, None] == node_iota[None, :]).astype(jnp.float32)
    node_counts = jnp.sum(membership, axis=0)
    node_sums = jnp.dot(
        membership.T,
        label_encoded,
        precision=lax.Precision.HIGHEST,
        preferred_element_type=jnp.float32,
    )
    head_rows = (node_sums / node_counts[:, None] + free_vectors.astype(jnp.float32)).astype(
        jnp.bfloat16
    )
    positive_owner = positives // label_count
    positive_node = jnp.take(label_node, positives)
    matches = (shortlist_owner[:, :, None, None] == positive_owner[:, None, None, :]) & (
        shortlist_node[:, :, :, None] == positive_node[:, None, None, :]
    )
    targets = jnp.any(matches, axis=3).astype(jnp.float32)
    flat_owner = shortlist_owner.reshape(-1)
    owner_table = (flat_owner[:, None] == jnp.arange(devices, dtype=jnp.int32)[None, :]).astype(
        jnp.int32
    )
    slot_rank = jnp.sum(jnp.cumsum(owner_table, axis=0) * owner_table, axis=1) - 1
    outgoing = (
        jnp.zeros((devices, CAP, model_width), jnp.bfloat16)
        .at[flat_owner, slot_rank]
        .set(jnp.repeat(query_rows, owners_each, axis=0))
    )
    entry_codes = (shortlist_node.astype(jnp.float32) + node_count * targets).reshape(
        -1, listed_count
    )
    code_slots = (
        jnp.full((devices, CAP, listed_count), -1.0, jnp.bfloat16)
        .at[flat_owner, slot_rank]
        .set(entry_codes.astype(jnp.bfloat16))
    )
    arrived, arrived_codes = (
        lax.all_to_all(outgoing, ("lab", "leaf"), split_axis=0, concat_axis=0, tiled=True),
        lax.all_to_all(code_slots, ("lab", "leaf"), split_axis=0, concat_axis=0, tiled=True),
    )
    arrived = arrived.reshape(-1, model_width)
    slot_codes = arrived_codes.reshape(-1, listed_count).astype(jnp.float32)
    live_slot = (slot_codes >= 0.0).astype(jnp.float32)
    slot_targets = (slot_codes >= node_count).astype(jnp.float32)
    node_local = slot_codes - node_count * slot_targets
    selector = (node_local[:, :, None] == node_iota[None, None, :].astype(jnp.float32)).astype(
        jnp.float32
    )
    slot_scores = SCORE_SCALE * jnp.dot(arrived, head_rows.T, preferred_element_type=jnp.float32)
    scores = jnp.sum(selector * slot_scores[:, None, :], axis=2)
    part_loss = jnp.sum(live_slot * (jax.nn.softplus(scores) - slot_targets * scores), axis=1)
    coefficient = SCORE_SCALE * (jax.nn.sigmoid(scores) - slot_targets) * live_slot
    weighting = jnp.sum(coefficient[:, :, None] * selector, axis=1).astype(jnp.bfloat16)
    back_grad = jnp.dot(weighting, head_rows, preferred_element_type=jnp.float32)
    grad_free = jnp.dot(weighting.T, arrived, preferred_element_type=jnp.float32)
    returned, returned_loss = (
        lax.all_to_all(
            back_grad.reshape(devices, CAP, model_width),
            ("lab", "leaf"),
            split_axis=0,
            concat_axis=0,
            tiled=True,
        ),
        lax.all_to_all(
            part_loss.reshape(devices, CAP),
            ("lab", "leaf"),
            split_axis=0,
            concat_axis=0,
            tiled=True,
        ),
    )
    query_grad = (
        returned[flat_owner, slot_rank].reshape(query_count, owners_each, model_width).sum(axis=1)
    )
    query_loss = returned_loss[flat_owner, slot_rank].reshape(query_count, owners_each).sum(axis=1)
    label_grad = jnp.dot(
        membership,
        grad_free / node_counts[:, None],
        precision=lax.Precision.HIGHEST,
        preferred_element_type=jnp.float32,
    )
    grad_encoded = jnp.concatenate([query_grad, label_grad], axis=0)
    grad_three, grad_five, grad_projection = backward_pass(
        three_taps,
        five_taps,
        preact,
        pooled,
        grad_encoded,
        projection,
        width_three_filters.shape[1],
        length,
    )
    summed = lax.psum((grad_three, grad_five, grad_projection), ("lab", "leaf"))
    leaf_index = lax.axis_index("leaf")
    outputs = tuple(
        (
            lax.dynamic_slice_in_dim(
                reduced,
                leaf_index * (reduced.shape[0] // leaf_count),
                reduced.shape[0] // leaf_count,
                0,
            )
            for reduced in summed
        )
    )
    return (query_loss, grad_free, outputs[0], outputs[1], outputs[2])


def solution(mesh):
    in_specs = (
        P(("lab", "leaf"), None),
        P(("lab", "leaf"), None),
        P(),
        P(("lab", "leaf"), None),
        P(("lab", "leaf"), None, None),
        P(("lab", "leaf"), None),
        P(),
        P(),
        P(),
        P(),
        P(("lab", "leaf"), None),
    )
    out_specs = (
        P(("lab", "leaf")),
        P(("lab", "leaf"), None),
        P("leaf", None),
        P("leaf", None),
        P("leaf", None),
    )
    return jax.shard_map(
        per_device, mesh=mesh, in_specs=in_specs, out_specs=out_specs, check_vma=False
    )
```

profile of v0, /device:TPU:1, one launch (start us, length us, event | category | flops | bytes accessed | tf_op | source)
XLA Modules:
  0.0 380.0 jit_solution(2863756976833752459)
XLA Ops:
  7.2 0.9 copy.110
  9.9 1.1 gather_fusion
  12.2 25.9 %scatter_fusion = bf16[128,8,8]{2,1,0:T(8,128)(2,1)} fusion(bf16[128,8,8]{2,1,0:T(8,128)(2,1)} %broadcast_in_dim.25, s32[256]{0:T(256)S(1)} %bitcast.80, bf16[256,8]{1,0:T(8,128)(2,1)S(1)} %bitcast.99), kind=kCustom, calls=%fused_computation.4 | custom fusion | bytes 14336 | tf_op jit(solution)/shard_map/scatter | solution.py:123
  38.1 11.4 %all-to-all-start = ((bf16[128,8,8]{2,1,0:T(8,128)(2,1)}), bf16[128,8,8]{2,1,0:T(8,128)(2,1)S(1)}, u32[]{:S(2)}, u32[]{:S(2)}) async-start(bf16[128,8,8]{2,1,0:T(8,128)(2,1)} %scatter_fusion), calls=%async_computation | async-start | bytes 524288 | tf_op jit(solution)/shard_map/all_to_all | solution.py:127
  50.0 17.7 %gather_fusion.3 = bf16[3072,256]{1,0:T(8,128)(2,1)S(1)} fusion(bf16[32768,256]{1,0:T(8,128)(2,1)} %param.19, s32[3072]{0:T(1024)S(1)} %broadcast_clamp_fusion), kind=kCustom, calls=%fused_computation.clone | custom fusion | bytes 3158016 | tf_op jit(solution)/shard_map/jit(_take)/gather | solution.py:14
  68.9 1.5 pad_slice_fusion.1
  71.0 0.8 fusion.24
  72.6 4.4 %fusion.62 = f32[3072,512]{1,0:T(8,128)S(1)} fusion(bf16[3072,1280]{1,0:T(8,128)(2,1)S(1)} %bitcast.95, bf16[1280,512]{1,0:T(8,128)(2,1)S(1)} %copy-done), kind=kOutput, calls=%fused_computation.136 | convolution fusion | flops 4026531840 | bytes 15466496 | tf_op jit(solution)/shard_map/dot_general | solution.py:34
  77.7 1.1 copy-done.18
  78.8 2.6 fusion.61
  81.4 4.8 %fusion.17 = f32[96,1024]{1,0:T(8,128)S(1)} fusion(f32[96,32,512]{2,1,0:T(8,128)S(1)} %bitcast.84, f32[96,32,512]{2,1,0:T(8,128)S(1)} %bitcast.85), kind=kLoop, calls=%fused_computation.29 | loop fusion | flops 31358976 | bytes 12976128 | tf_op jit(solution)/shard_map/reduce_sum | solution.py:38
  87.1 1.1 broadcast_in_dim.28
  88.2 32.4 %scatter_fusion.1 = bf16[128,8,512]{2,1,0:T(8,128)(2,1)} fusion(bf16[128,8,512]{2,1,0:T(8,128)(2,1)} %broadcast_in_dim.28, s32[256]{0:T(256)S(1)} %bitcast.81, bf16[256,512]{1,0:T(8,128)(2,1)S(1)} %broadcast_bitcast_fusion), kind=kCustom, calls=%fused_computation.5 | custom fusion | bytes 788480 | tf_op jit(solution)/shard_map/scatter | solution.py:115
  120.7 9.8 %all-to-all-start.1 = ((bf16[128,8,512]{2,1,0:T(8,128)(2,1)}), bf16[128,8,512]{2,1,0:T(8,128)(2,1)S(1)}, u32[]{:S(2)}, u32[]{:S(2)}) async-start(bf16[128,8,512]{2,1,0:T(8,128)(2,1)} %scatter_fusion.1), calls=%async_computation.1 | async-start | bytes 2097152 | tf_op jit(solution)/shard_map/all_to_all | solution.py:126
  131.0 18.2 %all-to-all-done.1 = bf16[128,8,512]{2,1,0:T(8,128)(2,1)S(1)} async-done(((bf16[128,8,512]{2,1,0:T(8,128)(2,1)}), bf16[128,8,512]{2,1,0:T(8,128)(2,1)S(1)}, u32[]{:S(2)}, u32[]{:S(2)}) %all-to-all-start.1) | async-done | bytes 1048608 | tf_op jit(solution)/shard_map/all_to_all | solution.py:126
  149.9 1.8 convolution_bitcast_fusion
  151.8 4.8 %all-to-all-start.3 = ((f32[128,8,512]{2,1,0:T(8,128)}), f32[128,8,512]{2,1,0:T(8,128)S(1)}, u32[]{:S(2)}, u32[]{:S(2)}) async-start(f32[128,8,512]{2,1,0:T(8,128)} %convolution_bitcast_fusion), calls=%async_computation.3 | async-start | bytes 4194304 | tf_op jit(solution)/shard_map/all_to_all | solution.py:145
  157.1 29.3 %all-to-all-done.3 = f32[128,8,512]{2,1,0:T(8,128)S(1)} async-done(((f32[128,8,512]{2,1,0:T(8,128)}), f32[128,8,512]{2,1,0:T(8,128)S(1)}, u32[]{:S(2)}, u32[]{:S(2)}) %all-to-all-start.3) | async-done | bytes 2097184 | tf_op jit(solution)/shard_map/all_to_all | solution.py:145
  186.4 1.5 gather_fusion.2
  188.0 1.8 convolution_multiply_fusion
  189.9 11.6 %fusion.6 = bf16[3072,1024]{1,0:T(8,128)(2,1)S(1)} fusion(f32[3072,512]{1,0:T(8,128)} %copy-done.3, f32[3072,512]{1,0:T(8,128)} %copy-done.4, f32[96,1024]{1,0:T(8,128)S(1)} %convolution_multiply_fusion), kind=kLoop, calls=%fused_computation.17 | loop fusion | flops 66060288 | bytes 19267584 | tf_op jit(solution)/shard_map/convert_element_type | solution.py:51
  201.6 3.8 fusion.20
  205.4 5.8 %fusion.18 = f32[1280,512]{1,0:T(8,128)} fusion(bf16[3072,1280]{1,0:T(8,128)(2,1)S(1)} %bitcast.98, bf16[3072,1024]{1,0:T(8,128)(2,1)S(1)} %fusion.6), kind=kOutput, calls=%fused_computation.31 | convolution fusion | flops 4026531840 | bytes 13631488 | tf_op jit(solution)/shard_map/dot_general | solution.py:55
  211.2 1.8 fusion.44
  213.3 1.1 fusion.35
  214.4 4.8 %all-to-all-start.2 = ((f32[128,1,8]{2,1,0:T(1,128)}), f32[128,1,8]{2,1,0:T(1,128)S(1)}, u32[]{:S(2)}, u32[]{:S(2)}) async-start(f32[128,1,8]{2,1,0:T(1,128)} %bitcast.16), calls=%async_computation.2 | async-start | bytes 131072 | tf_op jit(solution)/shard_map/all_to_all | solution.py:152
  219.2 9.5 %all-to-all-done.2 = f32[128,1,8]{2,1,0:T(1,128)S(1)} async-done(((f32[128,1,8]{2,1,0:T(1,128)}), f32[128,1,8]{2,1,0:T(1,128)S(1)}, u32[]{:S(2)}, u32[]{:S(2)}) %all-to-all-start.2) | async-done | bytes 4128 | tf_op jit(solution)/shard_map/all_to_all | solution.py:152
  228.7 1.9 gather_fusion.1
  231.4 137.0 %all-reduce.5.cloned.1.call-done = (f32[768,512]{1,0:T(8,128)}, f32[1280,512]{1,0:T(8,128)}, f32[1024,512]{1,0:T(8,128)}) async-done(((f32[768,512]{1,0:T(8,128)}, f32[1280,512]{1,0:T(8,128)}, f32[1024,512]{1,0:T(8,128)}), (f32[768,512]{1,0:T(8,128)}, f32[1280,512]{1,0:T(8,128)}, f32[1024,512]{1,0:T(8,128)})) %all-reduce.5.cloned.1.call-update) | async-done | bytes 6291472 | tf_op jit(solution)/shard_map/psum | solution.py:181
  368.4 1.5 constant_dynamic-slice_fusion.2
  370.0 1.6 constant_dynamic-slice_fusion.1
  371.6 1.6 constant_dynamic-slice_fusion
  (109 shorter events, 10.1 us)
Async XLA Ops:
  7.2 65.4 %copy-start = (bf16[1280,512]{1,0:T(8,128)(2,1)S(1)}, bf16[1280,512]{1,0:T(8,128)(2,1)}, u32[]{:S(2)}) copy-start(bf16[1280,512]{1,0:T(8,128)(2,1)} %param.21) | copy-start | bytes 3932164
  7.2 2.7 copy-start.2
  9.9 1.4 copy-start.17
  9.9 1.4 copy-start.14
  9.9 1.4 copy-start.12
  9.9 39.6 %copy-start.15 = (s32[32,32]{1,0:T(8,128)S(1)}, s32[32,32]{1,0:T(8,128)}, u32[]{:S(2)}) copy-start(s32[32,32]{1,0:T(8,128)} %param.13) | copy-start | bytes 12292
  9.9 39.7 %copy-start.16 = (s32[64,32]{0,1:T(8,128)S(1)}, s32[64,32]{0,1:T(8,128)}, u32[]{:S(2)}) copy-start(s32[64,32]{0,1:T(8,128)} %param.14) | copy-start | bytes 24580
  38.1 82.5 %all-to-all-start = ((bf16[128,8,8]{2,1,0:T(8,128)(2,1)}), bf16[128,8,8]{2,1,0:T(8,128)(2,1)S(1)}, u32[]{:S(2)}, u32[]{:S(2)}) async-start(bf16[128,8,8]{2,1,0:T(8,128)(2,1)} %scatter_fusion), calls=%async_computation | async-start | bytes 524288 | tf_op jit(solution)/shard_map/all_to_all | solution.py:127
  72.6 4.5 %copy-start.11 = (bf16[96,32,1280]{2,1,0:T(8,128)(2,1)}, bf16[96,32,1280]{2,1,0:T(8,128)(2,1)S(1)}, u32[]{:S(2)}) copy-start(bf16[96,32,1280]{2,1,0:T(8,128)(2,1)S(1)} %fusion.25) | copy-start | bytes 23592964
  77.1 4.3 %copy-start.3 = (f32[3072,512]{1,0:T(8,128)}, f32[3072,512]{1,0:T(8,128)S(1)}, u32[]{:S(2)}) copy-start(f32[3072,512]{1,0:T(8,128)S(1)} %fusion.62) | copy-start | bytes 18874372
  77.1 1.7 copy-start.18
  77.7 3.7 copy-start.5
  81.4 4.9 %copy-start.4 = (f32[3072,512]{1,0:T(8,128)}, f32[3072,512]{1,0:T(8,128)S(1)}, u32[]{:S(2)}) copy-start(f32[3072,512]{1,0:T(8,128)S(1)} %fusion.61) | copy-start | bytes 18874372
  81.4 4.8 %copy-start.6 = (bf16[1024,512]{1,0:T(8,128)(2,1)S(1)}, bf16[1024,512]{1,0:T(8,128)(2,1)}, u32[]{:S(2)}) copy-start(bf16[1024,512]{1,0:T(8,128)(2,1)} %param.22) | copy-start | bytes 3145732
  86.3 0.8 copy-start.7
  86.3 44.3 %copy-start.19 = (bf16[16,512]{1,0:T(8,128)(2,1)S(1)}, bf16[16,512]{1,0:T(8,128)(2,1)}, u32[]{:S(2)}) copy-start(bf16[16,512]{1,0:T(8,128)(2,1)} %param.23) | copy-start | bytes 49156
  120.7 31.1 %copy-start.9 = (bf16[128,8,8]{2,1,0:T(8,128)(2,1)}, bf16[128,8,8]{2,1,0:T(8,128)(2,1)S(1)}, u32[]{:S(2)}) copy-start(bf16[128,8,8]{2,1,0:T(8,128)(2,1)S(1)} %all-to-all-done) | copy-start | bytes 49156
  120.7 28.6 %all-to-all-start.1 = ((bf16[128,8,512]{2,1,0:T(8,128)(2,1)}), bf16[128,8,512]{2,1,0:T(8,128)(2,1)S(1)}, u32[]{:S(2)}, u32[]{:S(2)}) async-start(bf16[128,8,512]{2,1,0:T(8,128)(2,1)} %scatter_fusion.1), calls=%async_computation.1 | async-start | bytes 2097152 | tf_op jit(solution)/shard_map/all_to_all | solution.py:126
  151.8 34.6 %all-to-all-start.3 = ((f32[128,8,512]{2,1,0:T(8,128)}), f32[128,8,512]{2,1,0:T(8,128)S(1)}, u32[]{:S(2)}, u32[]{:S(2)}) async-start(f32[128,8,512]{2,1,0:T(8,128)} %convolution_bitcast_fusion), calls=%async_computation.3 | async-start | bytes 4194304 | tf_op jit(solution)/shard_map/all_to_all | solution.py:145
  156.5 211.9 %all-reduce.5.cloned.1.call-start = ((), (), s32[]{:S(2)}) async-start(), calls=%async_computation.4 | async-start | bytes 12582912 | tf_op jit(solution)/shard_map/psum | solution.py:181
  156.8 44.7 %copy-start.13 = (f32[16,512]{1,0:T(8,128)}, f32[16,512]{1,0:T(8,128)S(1)}, u32[]{:S(2)}) copy-start(f32[16,512]{1,0:T(8,128)S(1)} %fusion.28) | copy-start | bytes 98308
  188.0 13.5 %slice-start = ((s8[4718592]{0:T(1024)(128)(4,1)}), s8[4194304]{0:T(1024)(128)(4,1)S(1)}, s32[]{:S(2)}) async-start(s8[4718592]{0:T(1024)(128)(4,1)} %bitcast.90), calls=%async_computation.5 | async-start | bytes 8388608
  188.0 17.4 %slice-start.2 = ((s8[7864320]{0:T(1024)(128)(4,1)}), s8[4194304]{0:T(1024)(128)(4,1)S(1)}, s32[]{:S(2)}) async-start(s8[7864320]{0:T(1024)(128)(4,1)} %bitcast.96), calls=%async_computation.7 | async-start | bytes 8388608
  189.9 11.7 %slice-start.1 = ((s8[4718592]{0:T(1024)(128)(4,1)}), s8[524288]{0:T(1024)(128)(4,1)S(1)}, s32[]{:S(2)}) async-start(s8[4718592]{0:T(1024)(128)(4,1)} %bitcast.90), calls=%async_computation.6 | async-start | bytes 1048576
  189.9 15.5 %slice-start.3 = ((s8[7864320]{0:T(1024)(128)(4,1)}), s8[3670016]{0:T(1024)(128)(4,1)S(1)}, s32[]{:S(2)}) async-start(s8[7864320]{0:T(1024)(128)(4,1)} %bitcast.96), calls=%async_computation.8 | async-start | bytes 7340032
  205.4 5.9 %copy-start.8 = (f32[96,1024]{1,0:T(8,128)S(1)}, f32[96,1024]{1,0:T(8,128)}, u32[]{:S(2)}) copy-start(f32[96,1024]{1,0:T(8,128)} %copy-done.7) | copy-start | bytes 1179652
  205.4 167.8 %copy-start.1 = (bf16[1280,512]{1,0:T(8,128)(2,1)S(1)}, bf16[1280,512]{1,0:T(8,128)(2,1)}, u32[]{:S(2)}) copy-start(bf16[1280,512]{1,0:T(8,128)(2,1)} %param.21) | copy-start | bytes 3932164
  211.2 2.1 copy-start.10
  214.4 14.3 %all-to-all-start.2 = ((f32[128,1,8]{2,1,0:T(1,128)}), f32[128,1,8]{2,1,0:T(1,128)S(1)}, u32[]{:S(2)}, u32[]{:S(2)}) async-start(f32[128,1,8]{2,1,0:T(1,128)} %bitcast.16), calls=%async_computation.2 | async-start | bytes 131072 | tf_op jit(solution)/shard_map/all_to_all | solution.py:152
Sparse Core Ops, SparseCore 0:
  213.2 155.1 all-reduce.4
where the time goes:
time: 382 us; the launch traced here: 380 us
  waiting for transfers between devices  194 us (51%)
  local copies, waits for them, and re-layouts  95.1 us (25%)
  starting transfers between devices  30.7 us (8%)
  matrix products  23.5 us (6%)
  other arithmetic  21.9 us (6%)
  between operations  14.7 us (4%)
    psum x1, waiting for transfers between devices, per_device(): summed = lax.psum((grad_three, grad_five, grad_projection), ('lab', 'leaf'))  137 us
    scatter x1, local copies, waits for them, and re-layouts, per_device(): outgoing = jnp.zeros((devices, CAP, model_width), jnp.bfloat16).at[flat_o...  32.4 us
    all_to_all x1, waiting for transfers between devices, per_device(): lax.all_to_all(back_grad.reshape(devices, CAP, model_width), ('lab', 'lea...  29.3 us
    scatter x1, local copies, waits for them, and re-layouts, per_device(): code_slots = jnp.full((devices, CAP, listed_count), -1.0, jnp.bfloat16).a...  25.9 us
    all_to_all x1, waiting for transfers between devices, per_device(): lax.all_to_all(outgoing, ('lab', 'leaf'), split_axis=0, concat_axis=0, ti...  18.2 us
    gather x1, local copies, waits for them, and re-layouts, unfold(): embedded = jnp.take(token_lookup_table, token_numbers, axis=0)  17.7 us
    convert_element_type x1, other arithmetic, backward_pass(): grad_preact = pullback(spread)[0].astype(jnp.bfloat16)  11.6 us
    all_to_all x1, starting transfers between devices, per_device(): lax.all_to_all(code_slots, ('lab', 'leaf'), split_axis=0, concat_axis=0,...  11.4 us
  transfers between devices with their start and end apart: 5, of which 4 were waited for; matrix products, arithmetic and copies ran while one was open for 20% of the time, Pallas kernels for 0%

commit v1 on v0

v1 whole, which is shorter than its diff:
```python
import jax
import jax.numpy as jnp
from jax import lax
from jax.sharding import PartitionSpec as P

SCORE_SCALE = 0.25


def gelu_tanh(values):
    return jax.nn.gelu(values, approximate=True)


def per_device(
    query_tokens,
    label_tokens,
    label_node,
    shortlist_owner,
    shortlist_node,
    positives,
    table,
    three,
    five,
    projection,
    free_vectors,
):
    axes = ("lab", "leaf")
    leaf_count = lax.axis_size("leaf")
    devices = lax.axis_size("lab") * leaf_count
    device_index = lax.axis_index("lab") * leaf_count + lax.axis_index("leaf")
    query_count, length = query_tokens.shape
    label_count = label_tokens.shape[0]
    node_count, width = free_vectors.shape
    emb = table.shape[1]
    channels = three.shape[1]
    nodes = devices * node_count
    titles = query_count + label_count

    listed = (shortlist_owner[:, :, None] * node_count + shortlist_node).reshape(query_count, -1)
    home = positives // label_count * node_count + jnp.take(label_node, positives)
    node_iota = jnp.arange(nodes, dtype=jnp.int32)
    is_listed = jnp.any(listed[:, :, None] == node_iota[None, None, :], axis=1)
    is_home = jnp.any(home[:, :, None] == node_iota[None, None, :], axis=1)
    code = is_listed.astype(jnp.bfloat16) * (1 + is_home.astype(jnp.bfloat16))
    code_out = code.reshape(query_count, devices, node_count).transpose(1, 2, 0)
    code_in = lax.all_to_all(code_out, axes, split_axis=0, concat_axis=0, tiled=True)
    owner_code = code_in.transpose(1, 0, 2).reshape(node_count, devices * query_count)

    tokens = jnp.concatenate([query_tokens, label_tokens], axis=0).T.reshape(-1)
    embedded = jnp.take(table, tokens, axis=0)
    margin = 2 * titles
    padded = jnp.pad(embedded, ((margin, margin), (0, 0)))
    rows = length * titles

    def taps(offset):
        return lax.slice_in_dim(padded, margin + offset * titles, margin + offset * titles + rows)

    five_taps = jnp.concatenate([taps(o) for o in (-2, -1, 0, 1, 2)], axis=1)
    three_taps = five_taps[:, emb : 4 * emb]
    pre3 = jnp.dot(three_taps, three, preferred_element_type=jnp.float32)
    pre5 = jnp.dot(five_taps, five, preferred_element_type=jnp.float32)

    def pool(v):
        return jnp.mean(gelu_tanh(v).reshape(length, titles, -1), axis=0).astype(jnp.bfloat16)

    pooled = jnp.concatenate([pool(pre3), pool(pre5)], axis=1)
    encoded = jnp.dot(pooled, projection, preferred_element_type=jnp.float32)
    query_rows = encoded[:query_count].astype(jnp.bfloat16)
    all_queries = lax.all_gather(query_rows, axes, axis=0, tiled=True)

    own_nodes = lax.dynamic_slice_in_dim(label_node, device_index * label_count, label_count)
    membership = (own_nodes[:, None] == jnp.arange(node_count, dtype=jnp.int32)[None, :]).astype(
        jnp.float32
    )
    counts = jnp.sum(membership, axis=0)
    sums = jnp.dot(
        membership.T,
        encoded[query_count:],
        precision=lax.Precision.HIGHEST,
        preferred_element_type=jnp.float32,
    )
    head_rows = (sums / counts[:, None] + free_vectors.astype(jnp.float32)).astype(jnp.bfloat16)
    all_heads = lax.all_gather(head_rows, axes, axis=0, tiled=True)

    def weigh(scores, code):
        target = (code > 1.5).astype(jnp.float32)
        live = (code > 0.5).astype(jnp.float32)
        coefficient = SCORE_SCALE * (jax.nn.sigmoid(scores) - target) * live
        return live, target, coefficient.astype(jnp.bfloat16)

    def dot_t(a, b):
        return lax.dot_general(a, b, (((1,), (1,)), ((), ())), preferred_element_type=jnp.float32)

    own_scores = SCORE_SCALE * dot_t(head_rows, all_queries)
    _, _, own_weights = weigh(own_scores, owner_code.astype(jnp.float32))
    grad_free = jnp.dot(own_weights, all_queries, preferred_element_type=jnp.float32)
    scores = SCORE_SCALE * dot_t(query_rows, all_heads)
    live, target, weights = weigh(scores, code.astype(jnp.float32))
    query_loss = jnp.sum(live * (jax.nn.softplus(scores) - target * scores), axis=1)
    query_grad = jnp.dot(weights, all_heads, preferred_element_type=jnp.float32)

    label_up = jnp.dot(
        membership.astype(jnp.bfloat16),
        (grad_free / counts[:, None]).astype(jnp.bfloat16),
        preferred_element_type=jnp.float32,
    ).astype(jnp.bfloat16)
    upstream = jnp.concatenate([query_grad.astype(jnp.bfloat16), label_up], axis=0)
    grad_projection = jnp.dot(pooled.T, upstream, preferred_element_type=jnp.float32)
    grad_pooled = dot_t(upstream, projection) / length

    def back(pre, part):
        pullback = jax.vjp(gelu_tanh, pre)[1]
        spread = jnp.broadcast_to(part[None], (length,) + part.shape).reshape(pre.shape)
        return pullback(spread)[0].astype(jnp.bfloat16)

    g3 = back(pre3, grad_pooled[:, :channels])
    g5 = back(pre5, grad_pooled[:, channels:])

    def finish(partial):
        part = lax.psum_scatter(partial, "leaf", scatter_dimension=0, tiled=True)
        return lax.psum(part, "lab")

    grad_three = jnp.dot(three_taps.T, g3, preferred_element_type=jnp.float32)
    grad_five = jnp.dot(five_taps.T, g5, preferred_element_type=jnp.float32)
    return (query_loss, grad_free, finish(grad_three), finish(grad_five), finish(grad_projection))


def solution(mesh):
    both = ("lab", "leaf")
    in_specs = (
        P(both, None),
        P(both, None),
        P(),
        P(both, None),
        P(both, None, None),
        P(both, None),
        P(),
        P(),
        P(),
        P(),
        P(both, None),
    )
    out_specs = (P(both), P(both, None), P("leaf", None), P("leaf", None), P("leaf", None))
    return jax.shard_map(
        per_device, mesh=mesh, in_specs=in_specs, out_specs=out_specs, check_vma=False
    )
```

time: 382 us -> 514 us (1.35)
  waiting for transfers between devices: 194 us -> 366 us
  local copies, waits for them, and re-layouts: 95.1 us -> 35 us
  starting transfers between devices: 30.7 us -> 0.69 us
  blocking collectives: 0 us -> 21.5 us
  matrix products: 23.5 us -> 44.6 us
  other arithmetic: 21.9 us -> 30.3 us
    reduce_scatter x0 -> x3, waiting for transfers between devices: none -> 207 us  [finish(): part = lax.psum_scatter(partial, 'leaf', scatter_dimension=0, tiled=True)]
    all_gather x0 -> x2, waiting for transfers between devices: none -> 96.5 us  [the longest x1 62.8 us: per_device(): all_queries = lax.all_gather(query_rows, axes, axis=0, tiled=True)]
    psum x1, waiting for transfers between devices: 137 us -> 62.4 us  [finish(): return lax.psum(part, 'lab')]
    scatter x2 -> x0, local copies, waits for them, and re-layouts: 58.3 us -> none  [the longest x1 32.4 us: per_device(): outgoing = jnp.zeros((devices, CAP, model_width), jnp.bfloat16).at[flat_o...]
    all_to_all x4 -> x0, waiting for transfers between devices: 57 us -> none  [the longest x1 29.3 us: per_device(): lax.all_to_all(back_grad.reshape(devices, CAP, model_width), ('lab', 'lea...]
    all_to_all x4 -> x0, starting transfers between devices: 30.7 us -> none  [the longest x1 11.4 us: per_device(): lax.all_to_all(code_slots, ('lab', 'leaf'), split_axis=0, concat_axis=0,...]
    all_to_all x0 -> x1, blocking collectives: none -> 21.5 us  [per_device(): lax.all_to_all(code_out, axes, split_axis=0, concat_axis=0, tiled=True)]
    dot_general x12, matrix products: 23.5 us -> 44.6 us  [the longest x1 11.4 us: per_device(): pre5 = jnp.dot(five_taps, five, preferred_element_type=jnp.float32)]
  transfers between devices with their start and end apart: 5 -> 6, of which waited for: 4 -> 6; matrix products, arithmetic and copies ran while one was open for 20% -> 7% of each run, Pallas kernels for 0% -> 0%
where the time goes in v1:
time: 514 us; the launch traced here: 513 us
  waiting for transfers between devices  366 us (71%)
  matrix products  44.6 us (9%)
  local copies, waits for them, and re-layouts  35 us (7%)
  other arithmetic  30.3 us (6%)
  blocking collectives  21.5 us (4%)
  between operations  14.7 us (3%)
    reduce_scatter x3, waiting for transfers between devices, finish(): part = lax.psum_scatter(partial, 'leaf', scatter_dimension=0, tiled=True)  207 us
    all_gather x1, waiting for transfers between devices, per_device(): all_queries = lax.all_gather(query_rows, axes, axis=0, tiled=True)  62.8 us
    psum x1, waiting for transfers between devices, finish(): return lax.psum(part, 'lab')  62.4 us
    all_gather x1, waiting for transfers between devices, per_device(): all_heads = lax.all_gather(head_rows, axes, axis=0, tiled=True)  33.6 us
    all_to_all x1, blocking collectives, per_device(): lax.all_to_all(code_out, axes, split_axis=0, concat_axis=0, tiled=True)  21.5 us
    gather x1, local copies, waits for them, and re-layouts, per_device(): embedded = jnp.take(table, tokens, axis=0)  20.1 us
    convert_element_type x2, other arithmetic, back(): return pullback(spread)[0].astype(jnp.bfloat16)  12.6 us
    dot_general x1, matrix products, per_device(): pre5 = jnp.dot(five_taps, five, preferred_element_type=jnp.float32)  11.4 us
  transfers between devices with their start and end apart: 6, of which 6 were waited for; matrix products, arithmetic and copies ran while one was open for 7% of the time, Pallas kernels for 0%

profile of v1, /device:TPU:1, one launch (start us, length us, event | category | flops | bytes accessed | tf_op | source)
XLA Modules:
  0.0 512.8 jit_solution(9845108619637096978)
XLA Ops:
  7.2 0.9 copy.53
  9.1 20.1 %gather_fusion.1 = bf16[3072,256]{1,0:T(8,128)(2,1)} fusion(bf16[32768,256]{1,0:T(8,128)(2,1)} %param.17, s32[3072]{0:T(1024)S(1)} %broadcast_clamp_fusion), kind=kCustom, calls=%fused_computation.1 | custom fusion | bytes 3158016 | tf_op jit(solution)/shard_map/jit(_take)/gather | solution.py:49
  29.3 2.8 broadcast_select_fusion
  32.3 1.6 constant_dynamic-update-slice_fusion.1
  34.4 7.3 %multiply_multiply_fusion.5 = (f32[3072,512]{1,0:T(8,128)}, f32[3072,512]{1,0:T(8,128)}) fusion(bf16[768,512]{1,0:T(8,128)(2,1)S(1)} %copy-done.23, bf16[3072,256]{1,0:T(8,128)(2,1)S(1)} %get-tuple-element.10, bf16[3072,256]{1,0:T(8,128)(2,1)S(1)} %broadcast_select_fusion, bf16[3072,256]{1,0:T(8,128)(2,1)S(1)} %get-tuple-element.8), kind=kOutput, calls=%fused_computation.33 | convolution fusion | flops 2442657792 | bytes 18087936 | tf_op jit(solution)/shard_map/dot_general | solution.py:59
  42.2 3.4 reduce_sum.36
  45.6 11.4 %multiply_multiply_fusion.4 = (f32[3072,512]{1,0:T(8,128)}, f32[3072,512]{1,0:T(8,128)}) fusion(bf16[3072,1280]{1,0:T(8,128)(2,1)} %copy-done.12, bf16[1280,512]{1,0:T(8,128)(2,1)S(1)} %copy-done), kind=kOutput, calls=%fused_computation.32 | convolution fusion | flops 4039114752 | bytes 21757952 | tf_op jit(solution)/shard_map/dot_general | solution.py:60
  57.0 3.5 reduce_sum.37
  63.2 1.1 gather_fusion
  64.9 4.2 fusion
  69.8 21.5 %all_to_all.5 = bf16[128,2,256]{2,1,0:T(2,128)(2,1)S(1)} all-to-all(bf16[128,2,256]{2,1,0:T(2,128)(2,1)S(1)} %reshape.115), channel_id=1, replica_groups=mesh['lab'=8,'leaf'=16] {'lab','leaf'}, dimensions={0} | all-to-all | bytes 262144 | tf_op jit(solution)/shard_map/all_to_all | solution.py:45
  91.6 0.9 convert_bitcast_fusion
  92.6 1.3 copy.56
  93.9 1.7 reshape.96
  95.6 1.1 copy.55
  97.3 33.6 %all-gather.3.cloned.1.call-done = bf16[2048,512]{1,0:T(8,128)(2,1)} async-done(((bf16[16,512]{1,0:T(8,128)(2,1)}), bf16[2048,512]{1,0:T(8,128)(2,1)}) %all-gather.3.cloned.1.call-update) | async-done | bytes 2097168 | tf_op jit(solution)/shard_map/all_gather | solution.py:82
  130.9 3.0 fusion.38
  134.0 2.1 convolution_convert_fusion.1
  136.1 62.8 %all-gather.5.cloned.1.call-done = bf16[4096,512]{1,0:T(8,128)(2,1)} async-done(((bf16[32,512]{1,0:T(8,128)(2,1)}), bf16[4096,512]{1,0:T(8,128)(2,1)}) %all-gather.5.cloned.1.call-update) | async-done | bytes 4194320 | tf_op jit(solution)/shard_map/all_gather | solution.py:68
  198.9 5.2 %fusion.31 = f32[16,512]{1,0:T(8,128)S(1)} fusion(bf16[4096,512]{1,0:T(8,128)(2,1)} %all-gather.5.cloned.1.call-done, pred[16,4096]{1,0:T(8,128)(4,1)S(1)} %gt.39, f32[16,4096]{1,0:T(8,128)S(1)} %reshape.96, bf16[16,512]{1,0:T(8,128)(2,1)S(1)} %copy-done.18), kind=kOutput, calls=%fused_computation.55 | convolution fusion | flops 134742016 | bytes 4571136 | tf_op jit(solution)/shard_map/dot_general | solution.py:95
  204.9 6.3 %fusion.7 = bf16[3072,512]{1,0:T(8,128)(2,1)S(1)} fusion(f32[3072,512]{1,0:T(8,128)} %get-tuple-element.18, f32[96,512]{1,0:T(8,128)S(1)} %get-tuple-element.14), kind=kLoop, calls=%fused_computation.18 | loop fusion | flops 31457280 | bytes 9633792 | tf_op jit(solution)/shard_map/convert_element_type | solution.py:113
  211.3 3.8 fusion.29
  215.2 1.8 fusion.46
  217.3 6.2 %fusion.14 = bf16[3072,512]{1,0:T(8,128)(2,1)S(1)} fusion(f32[3072,512]{1,0:T(8,128)} %get-tuple-element.16, f32[96,512]{1,0:T(8,128)S(1)} %get-tuple-element.13), kind=kLoop, calls=%fused_computation.25 | loop fusion | flops 31457280 | bytes 9633792 | tf_op jit(solution)/shard_map/convert_element_type | solution.py:113
  223.6 8.2 %fusion.70 = f32[1280,512]{1,0:T(8,128)} fusion(bf16[3072,1280]{1,0:T(8,128)(2,1)} %copy-done.12, bf16[3072,512]{1,0:T(8,128)(2,1)S(1)} %fusion.14), kind=kOutput, calls=%fused_computation.130 | convolution fusion | flops 4026531840 | bytes 13631488 | tf_op jit(solution)/shard_map/dot_general | solution.py:123
  231.8 52.4 %reduce-scatter.4.cloned.1.call-done = f32[48,512]{1,0:T(8,128)} async-done(((f32[768,512]{1,0:T(8,128)}), f32[48,512]{1,0:T(8,128)}) %reduce-scatter.4.cloned.1.call-update) | async-done | bytes 98320 | tf_op jit(solution)/shard_map/reduce_scatter | solution.py:119
  284.2 76.7 %reduce-scatter.8.cloned.1.call-done = f32[64,512]{1,0:T(8,128)} async-done(((f32[1024,512]{1,0:T(8,128)}), f32[64,512]{1,0:T(8,128)}) %reduce-scatter.8.cloned.1.call-update) | async-done | bytes 131088 | tf_op jit(solution)/shard_map/reduce_scatter | solution.py:119
  360.9 77.9 %reduce-scatter.6.cloned.1.call-done = f32[80,512]{1,0:T(8,128)} async-done(((f32[1280,512]{1,0:T(8,128)}), f32[80,512]{1,0:T(8,128)}) %reduce-scatter.6.cloned.1.call-update) | async-done | bytes 163856 | tf_op jit(solution)/shard_map/reduce_scatter | solution.py:119
  438.9 62.4 %all-reduce.4.cloned.1.call-done = (f32[48,512]{1,0:T(8,128)}, f32[80,512]{1,0:T(8,128)}, f32[64,512]{1,0:T(8,128)}) async-done(((f32[48,512]{1,0:T(8,128)}, f32[80,512]{1,0:T(8,128)}, f32[64,512]{1,0:T(8,128)}), (f32[48,512]{1,0:T(8,128)}, f32[80,512]{1,0:T(8,128)}, f32[64,512]{1,0:T(8,128)})) %all-reduce.4.cloned.1.call-update) | async-done | bytes 393232 | tf_op jit(solution)/shard_map/psum | solution.py:120
  501.2 1.5 copy.64
  502.8 1.6 copy.65
  504.4 1.6 copy.66
  (105 shorter events, 7.9 us)
Async XLA Ops:
  7.2 38.4 %copy-start = (bf16[1280,512]{1,0:T(8,128)(2,1)S(1)}, bf16[1280,512]{1,0:T(8,128)(2,1)}, u32[]{:S(2)}) copy-start(bf16[1280,512]{1,0:T(8,128)(2,1)} %param.19) | copy-start | bytes 3932164
  7.2 123.8 %all-gather.3.cloned.1.call-start = ((), (), s32[]{:S(2)}) async-start(), calls=%async_computation.4 | async-start | bytes 2113536 | tf_op jit(solution)/shard_map/all_gather | solution.py:82
  29.3 3.1 copy-start.3
  34.3 7.5 %copy-start.6 = (bf16[3072,256]{1,0:T(8,128)(2,1)}, bf16[3072,256]{1,0:T(8,128)(2,1)S(1)}, u32[]{:S(2)}) copy-start(bf16[3072,256]{1,0:T(8,128)(2,1)S(1)} %get-tuple-element.8) | copy-start | bytes 4718596
  34.3 7.5 %copy-start.8 = (bf16[3072,256]{1,0:T(8,128)(2,1)}, bf16[3072,256]{1,0:T(8,128)(2,1)S(1)}, u32[]{:S(2)}) copy-start(bf16[3072,256]{1,0:T(8,128)(2,1)S(1)} %get-tuple-element.10) | copy-start | bytes 4718596
  34.4 7.8 %copy-start.12 = (bf16[3072,1280]{1,0:T(8,128)(2,1)}, bf16[3072,1280]{1,0:T(8,128)(2,1)S(1)}, u32[]{:S(2)}) copy-start(bf16[3072,1280]{1,0:T(8,128)(2,1)S(1)} %slice_dynamic-update-slice_fusion) | copy-start | bytes 23592964
  57.0 3.5 copy-start.2
  57.0 3.8 copy-start.4
  57.0 4.1 copy-start.24
  57.0 5.9 %copy-start.22 = (s32[32,8]{0,1:T(8,128)S(1)}, s32[32,8]{0,1:T(8,128)}, u32[]{:S(2)}) copy-start(s32[32,8]{0,1:T(8,128)} %param.14) | copy-start | bytes 3076
  57.0 5.9 %copy-start.20 = (s32[32,8,8]{0,2,1:T(8,128)S(1)}, s32[32,8,8]{0,2,1:T(8,128)}, u32[]{:S(2)}) copy-start(s32[32,8,8]{0,2,1:T(8,128)} %param.15) | copy-start | bytes 24580
  57.0 6.0 %copy-start.21 = (s32[32,4]{0,1:T(4,128)S(1)}, s32[32,4]{0,1:T(4,128)}, u32[]{:S(2)}) copy-start(s32[32,4]{0,1:T(4,128)} %param.16) | copy-start | bytes 1540
  60.7 2.2 copy-start.27
  60.7 3.6 copy-start.10
  61.1 3.3 copy-start.13
  61.9 137.1 %all-gather.5.cloned.1.call-start = ((), (), s32[]{:S(2)}) async-start(), calls=%async_computation.5 | async-start | bytes 4227072 | tf_op jit(solution)/shard_map/all_gather | solution.py:68
  62.6 221.6 %reduce-scatter.4.cloned.1.call-start = ((), (), s32[]{:S(2)}) async-start(), calls=%async_computation.6 | async-start | bytes 1671168 | tf_op jit(solution)/shard_map/reduce_scatter | solution.py:119
  64.9 4.9 copy-start.16
  91.3 107.6 %copy-start.18 = (bf16[16,512]{1,0:T(8,128)(2,1)S(1)}, bf16[16,512]{1,0:T(8,128)(2,1)}, u32[]{:S(2)}) copy-start(bf16[16,512]{1,0:T(8,128)(2,1)} %fusion.33) | copy-start | bytes 49156
  92.6 41.4 %copy-start.15 = (pred[32,2048]{1,0:T(8,128)(4,1)S(1)}, pred[32,2048]{1,0:T(8,128)(4,1)}, u32[]{:S(2)}) copy-start(pred[32,2048]{1,0:T(8,128)(4,1)} %copy-done.14) | copy-start | bytes 196612
  92.6 41.4 %copy-start.17 = (pred[32,2048]{1,0:T(8,128)(4,1)S(1)}, pred[32,2048]{1,0:T(8,128)(4,1)}, u32[]{:S(2)}) copy-start(pred[32,2048]{1,0:T(8,128)(4,1)} %copy-done.16) | copy-start | bytes 196612
  133.9 70.2 %copy-start.26 = (s32[64]{0:T(128)S(1)}, s32[64]{0:T(128)}, u32[]{:S(2)}) copy-start(s32[64]{0:T(128)} %copy-done.25) | copy-start | bytes 772
  133.9 70.2 %copy-start.28 = (f32[16]{0:T(128)S(1)}, f32[16]{0:T(128)}, u32[]{:S(2)}) copy-start(f32[16]{0:T(128)} %copy-done.27) | copy-start | bytes 196
  133.9 70.5 %copy-start.5 = (bf16[1024,512]{1,0:T(8,128)(2,1)S(1)}, bf16[1024,512]{1,0:T(8,128)(2,1)}, u32[]{:S(2)}) copy-start(bf16[1024,512]{1,0:T(8,128)(2,1)} %param.20) | copy-start | bytes 3145732
  204.2 10.9 %copy-start.19 = (f32[16,512]{1,0:T(8,128)}, f32[16,512]{1,0:T(8,128)S(1)}, u32[]{:S(2)}) copy-start(f32[16,512]{1,0:T(8,128)S(1)} %fusion.31) | copy-start | bytes 98308
  204.2 7.1 %copy-start.7 = (bf16[3072,256]{1,0:T(8,128)(2,1)S(1)}, bf16[3072,256]{1,0:T(8,128)(2,1)}, u32[]{:S(2)}) copy-start(bf16[3072,256]{1,0:T(8,128)(2,1)} %copy-done.6) | copy-start | bytes 4718596
  204.2 7.1 %copy-start.9 = (bf16[3072,256]{1,0:T(8,128)(2,1)S(1)}, bf16[3072,256]{1,0:T(8,128)(2,1)}, u32[]{:S(2)}) copy-start(bf16[3072,256]{1,0:T(8,128)(2,1)} %copy-done.8) | copy-start | bytes 4718596
  211.3 3.9 copy-start.11
  215.1 145.8 %reduce-scatter.8.cloned.1.call-start = ((), (), s32[]{:S(2)}) async-start(), calls=%async_computation.8 | async-start | bytes 2228224 | tf_op jit(solution)/shard_map/reduce_scatter | solution.py:119
  217.0 221.8 %reduce-scatter.6.cloned.1.call-start = ((), (), s32[]{:S(2)}) async-start(), calls=%async_computation.7 | async-start | bytes 2785280 | tf_op jit(solution)/shard_map/reduce_scatter | solution.py:119
  217.3 288.6 %copy-start.1 = (bf16[1280,512]{1,0:T(8,128)(2,1)S(1)}, bf16[1280,512]{1,0:T(8,128)(2,1)}, u32[]{:S(2)}) copy-start(bf16[1280,512]{1,0:T(8,128)(2,1)} %param.19) | copy-start | bytes 3932164
  231.8 269.5 %all-reduce.4.cloned.1.call-start = ((), (), s32[]{:S(2)}) async-start(), calls=%async_computation.9 | async-start | bytes 786432 | tf_op jit(solution)/shard_map/psum | solution.py:120
  (3 other events, 4.8 us)
Sparse Core Ops, SparseCore 0:
  62.0 68.8 all-gather.2
  134.6 64.2 all-gather.4
  215.2 68.9 reduce-scatter.3
  287.4 73.4 reduce-scatter.7
  364.4 74.3 reduce-scatter.5
  441.4 59.8 all-reduce.3

commit v2 on v1

v2 whole, which is shorter than its diff:
```python
import jax
import jax.numpy as jnp
from jax import lax
from jax.experimental import pallas as pl
from jax.experimental.pallas import tpu as pltpu
from jax.sharding import PartitionSpec as P

MESH = pl.DeviceIdType.MESH
ORDERS = ("xyz", "yzx", "zxy")


SCORE_SCALE = 0.25


def where_am_i():
    lab, leaf = lax.axis_index("lab"), lax.axis_index("leaf")
    return {"z": lab // 2, "c": lab % 2, "y": leaf // 4, "x": leaf % 4}


def device_of(at):
    return (at["z"] * 2 + at["c"], at["y"] * 4 + at["x"])


def along(at, axis, step):
    size = 2 if axis == "c" else 4
    return {**at, axis: lax.rem(at[axis] + step, size)}


ROOT = 0.7978845608028654
CUBIC = 0.044715
Q_PARTS = ((0, 256), (256, 256), (512, 128))
H_PARTS = ((0, 128), (128, 128), (256, 256))
STEPS = (1, 3, 2)


def window_kernel(
    emb_ref, w3_hbm, w5_hbm, proj_hbm, info_ref, row_ref, col_ref, free_vec_ref,
    loss_ref, free_ref, out_ref,
    w3_ref, w5_ref, proj_ref, taps, slope, total, pooled_ref,
    all_q, all_h, free_acc, grad_acc, loss_acc, tiles,
    grad_pre, gp_ref, g5_ref, g3_ref,
    half, other, r1, b, r2, c, r3, done,
    load_sem, q_send, q_recv, h_send, h_recv, over_send, over_recv,
    core_send, core_recv, send_sem, recv_sem, out_send, out_recv, local_sem,
):
    at = where_am_i()
    bf16, f32 = jnp.bfloat16, jnp.float32
    core = at["c"]
    partner = along(at, "c", 1)
    lab_steps = [(z, cc) for z in range(4) for cc in range(2)][1:]
    lab_peers = [along(along(at, "z", z), "c", cc) for z, cc in lab_steps]
    home = (at["z"], at["c"], at["y"], at["x"])
    queries = info_ref.shape[0]
    labels = col_ref.shape[0]
    nodes, width = free_vec_ref.shape
    rows, emb = emb_ref.shape
    length = rows // (queries + labels)
    q_rows = queries * length
    channels = w3_ref.shape[1]
    wide = all_q.shape[-1]

    loads = [
        pltpu.make_async_copy(src, dst, load_sem.at[i])
        for i, (src, dst) in enumerate(((w3_hbm, w3_ref), (w5_hbm, w5_ref), (proj_hbm, proj_ref)))
    ]
    for load in loads:
        load.start()

    def nt(a, b):
        return lax.dot_general(a, b, (((1,), (1,)), ((), ())), preferred_element_type=f32)

    def tn(a, b):
        return lax.dot_general(a, b, (((0,), (0,)), ((), ())), preferred_element_type=f32)

    def unfold(base, titles):
        size = titles * length
        for k in range(5):
            move = (k - 2) * titles
            low, high = max(0, -move), size - max(0, move)
            columns = pl.ds(k * emb, emb)
            if low:
                taps[pl.ds(base, low), columns] = jnp.zeros((low, emb), bf16)
            taps[pl.ds(base + low, high - low), columns] = emb_ref[pl.ds(base + low + move, high - low), :]
            if high < size:
                taps[pl.ds(base + high, size - high), columns] = jnp.zeros((size - high, emb), bf16)

    def convolve(base, titles, first):
        block = 512
        for col in range(0, 2 * channels, 256):
            if col < channels:
                pre = jnp.dot(
                    taps[pl.ds(base, block), emb : 4 * emb], w3_ref[:, col : col + 256],
                    preferred_element_type=f32,
                )
            else:
                pre = jnp.dot(
                    taps[pl.ds(base, block), :], w5_ref[:, col - channels : col - channels + 256],
                    preferred_element_type=f32,
                )
            bend = (ROOT * CUBIC) * (pre * pre)
            inner = bend + ROOT
            tanh = jnp.tanh(pre * inner)
            gate = 1.0 + tanh
            value = pre * gate
            slope[pl.ds(base, block), col : col + 256] = gate + value * (1.0 - tanh) * (inner + (bend + bend))
            part = jnp.sum(value.reshape(block // titles, titles, 256), axis=0)
            where = pl.ds(0 if titles == queries else queries, titles)
            if first:
                total[where, col : col + 256] = part
            else:
                total[where, col : col + 256] += part

    def encoded_of(where):
        pooled = (total[where, :] * (0.5 / length)).astype(bf16)
        pooled_ref[where, :] = pooled
        return jnp.dot(pooled, proj_ref[...], preferred_element_type=f32)

    def region(ref, part, phase, place, columns, spread=slice(None)):
        free = ORDERS[part][:phase]
        z, y, x = [slice(None) if a in free else place[a] for a in "zyx"]
        return ref.at[z, place["c"], y, x, spread, pl.ds(*columns)]

    started = []

    def push(ref, send, recv, slot, peer):
        copy = pltpu.make_async_remote_copy(
            src_ref=ref,
            dst_ref=ref,
            send_sem=send.at[slot],
            recv_sem=recv.at[slot],
            device_id=device_of(peer),
            device_id_type=MESH,
        )
        copy.start()
        started.append(copy)
        return copy

    def direct(ref, columns, send, recv, part, phase):
        here = region(ref, part, phase, at, columns[part])
        axis = ORDERS[part][phase]
        return [
            push(here, send, recv, (part, phase * 3 + d - 1), along(at, axis, d)) for d in STEPS
        ]

    def hand_over(ref, columns, group, part, d):
        there = region(ref, part, 2, along(at, ORDERS[part][2], d), columns[part])
        return push(there, over_send, over_recv, (group, part * 4 + d), partner)

    def wait_all(copies):
        for copy in copies:
            copy.wait_recv()

    barrier = pltpu.get_barrier_semaphore()
    peers = [along(at, axis, d) for axis in "xy" for d in (1, 2, 3)] + lab_peers
    for peer in peers:
        pl.semaphore_signal(barrier, inc=1, device_id=device_of(peer), device_id_type=MESH)
    unfold(0, queries)
    loads[0].wait()
    loads[1].wait()
    convolve(0, queries, True)
    convolve(512, queries, False)
    unfold(q_rows, labels)
    loads[2].wait()
    all_q[(*home, slice(None), pl.ds(0, width))] = encoded_of(pl.ds(0, queries)).astype(bf16)
    all_q[(*home, slice(None), pl.ds(width, wide - width))] = info_ref[...]
    pl.semaphore_wait(barrier, len(peers))
    q_stage = [direct(all_q, Q_PARTS, q_send, q_recv, part, 0) for part in range(3)]
    over = []

    convolve(q_rows, labels, True)
    for part in range(3):
        wait_all(q_stage[part])
        q_stage[part] = direct(all_q, Q_PARTS, q_send, q_recv, part, 1)
    convolve(q_rows + 512, labels, False)
    near = []
    for part in range(3):
        wait_all(q_stage[part])
        here = region(all_q, part, 2, at, Q_PARTS[part])
        axis = ORDERS[part][2]
        near.append(
            [push(here, q_send, q_recv, (part, 6 + k), along(at, axis, d)) for k, d in ((0, 1), (1, 3))]
        )
        over.append(hand_over(all_q, Q_PARTS, 0, part, 0))
    convolve(q_rows + 1024, labels, False)
    convolve(q_rows + 1536, labels, False)
    label_encoded = encoded_of(pl.ds(queries, labels))
    member = lax.broadcasted_iota(jnp.int32, (nodes, labels), 0) == row_ref[...]
    member = jnp.where(member, 1.0, 0.0)
    counts = jnp.sum(member, axis=1, keepdims=True)
    sums = jnp.dot(member, label_encoded, precision=lax.Precision.HIGHEST, preferred_element_type=f32)
    heads = (sums / counts + free_vec_ref[...].astype(f32)).astype(bf16)
    all_h[home] = heads
    h_stage = [direct(all_h, H_PARTS, h_send, h_recv, part, 0) for part in range(3)]
    far = []
    for part in range(3):
        axis = ORDERS[part][2]
        wait_all(near[part])
        for k, d in ((2, 1), (3, 3)):
            spread = pl.ds((k - 2) * (queries // 2), queries // 2)
            there = region(all_q, part, 2, along(at, axis, 4 - d), Q_PARTS[part], spread)
            far.append(push(there, q_send, q_recv, (part, 6 + k), along(at, axis, d)))
        over.append(hand_over(all_q, Q_PARTS, 0, part, 3))
        over.append(hand_over(all_q, Q_PARTS, 0, part, 1))
    for part in range(3):
        wait_all(h_stage[part])
        h_stage[part] = direct(all_h, H_PARTS, h_send, h_recv, part, 1)

    info = info_ref[...].astype(f32)
    lane = lax.rem(lax.broadcasted_iota(jnp.int32, (queries, 128), 1), nodes).astype(f32)
    for k in range(8):
        tile = jnp.zeros((queries, 128), f32)
        for h in range(8):
            code = info[:, k * 8 + h : k * 8 + h + 1]
            tile += jnp.where(code == lane, 1.0, 0.0) + jnp.where(code == lane + nodes, 2.0, 0.0)
        tiles[k] = tile

    for part in range(3):
        wait_all(far[2 * part : 2 * part + 2])
        over.append(hand_over(all_q, Q_PARTS, 0, part, 2))
    h_over = []
    for part in range(3):
        wait_all(h_stage[part])
        h_stage[part] = direct(all_h, H_PARTS, h_send, h_recv, part, 2)
        h_over.append(hand_over(all_h, H_PARTS, 1, part, 0))
    wait_all(over)

    me = ((at["z"] * 2 + at["c"]) * 16 + at["y"] * 4 + at["x"]).astype(f32)
    fold_row = lax.broadcasted_iota(jnp.int32, (8, 128), 0)
    fold_col = lax.broadcasted_iota(jnp.int32, (8, 128), 1)
    fold = jnp.where((lax.rem(fold_col, 8) == fold_row) & (fold_col < 64), 1.0, 0.0).astype(bf16)
    free_acc[...] = jnp.zeros_like(free_acc)
    grad_acc[...] = jnp.zeros_like(grad_acc)
    loss_acc[...] = jnp.zeros_like(loss_acc)
    node = lax.broadcasted_iota(jnp.int32, (nodes, 512), 0).astype(f32) + 1.0

    @pl.loop(0, 8)
    def _(i):
        chunk = all_q[i // 2, i % 2].reshape(512, wide)
        keys = chunk[:, :width]
        note = chunk[:, width:].astype(f32)
        owner = pltpu.roll(note, 64, 1)
        mine = jnp.where(owner == me, note + 1.0, 0.0).astype(bf16)
        listed = nt(fold, mine)
        scores = SCORE_SCALE * nt(all_h[home], keys)
        live = jnp.zeros((nodes, 512), f32)
        target = jnp.zeros((nodes, 512), f32)
        for h in range(8):
            entry = listed[h : h + 1]
            hit = jnp.where(entry == node + nodes, 1.0, 0.0)
            target += hit
            live += jnp.where(entry == node, 1.0, hit)
        weight = (SCORE_SCALE * (jax.nn.sigmoid(scores) - target) * live).astype(bf16)
        free_acc[...] += jnp.dot(weight, keys, preferred_element_type=f32)

    for k, d in enumerate(STEPS):
        for part in range(3):
            h_stage[part][k].wait_recv()
            h_over.append(hand_over(all_h, H_PARTS, 1, part, 4 - d))
    wait_all(h_over)

    own_rows = all_q[(*home, slice(None), pl.ds(0, width))]

    @pl.loop(0, 8)
    def _(i):
        keys = all_h[i // 2, i % 2].reshape(256, width)
        scores = SCORE_SCALE * nt(own_rows, keys)
        place = (lax.broadcasted_iota(jnp.int32, (queries, 256), 1) // nodes + i * (256 // nodes)).astype(f32)
        code = jnp.zeros((queries, 256), f32)
        for k in range(8):
            tile = tiles[k]
            pair = jnp.concatenate([tile, tile], axis=1)
            code += jnp.where(info[:, 64 + k * 8 : 65 + k * 8] == place, pair, 0.0)
        target = jnp.where(code > 1.5, 1.0, 0.0)
        live = jnp.where(code > 0.5, 1.0, 0.0)
        small = jnp.exp(-jnp.abs(scores))
        softplus = jnp.maximum(scores, 0.0) + jnp.log1p(small)
        loss_acc[...] += live * (softplus - target * scores)
        weight = (SCORE_SCALE * (jax.nn.sigmoid(scores) - target) * live).astype(bf16)
        grad_acc[...] += jnp.dot(weight, keys, preferred_element_type=f32)

    loss_ref[...] = jnp.broadcast_to(jnp.sum(loss_acc[...], axis=1, keepdims=True), loss_ref.shape)
    free = free_acc[...]
    free_ref[...] = free
    spread = jnp.where(lax.broadcasted_iota(jnp.int32, (labels, nodes), 1) == col_ref[...], 1.0, 0.0)
    label_up = jnp.dot(spread.astype(bf16), (free / counts).astype(bf16), preferred_element_type=f32)
    upstream = jnp.concatenate([grad_acc[...].astype(bf16), label_up.astype(bf16)], axis=0)

    sent = []
    first = {}
    pieces = (
        (lambda k: gp_ref.at[:, :, k], 0, 0, 4),
        (lambda k: g5_ref.at[:, :, k, pl.ds(0, 4)], 1, 0, 4),
        (lambda k: g5_ref.at[:, :, k, pl.ds(4, 1)], 2, 0, 1),
        (lambda k: g3_ref.at[:, :, k], 2, 1, 3),
    )

    def swap(i):
        view, part, row, count = pieces[i]
        copy = pltpu.make_async_remote_copy(
            src_ref=view(1 - core),
            dst_ref=other.at[part, :, :, pl.ds(row, count)],
            send_sem=core_send.at[i],
            recv_sem=core_recv.at[i],
            device_id=device_of(partner),
            device_id_type=MESH,
        )
        copy.start()
        first[i] = copy
        sent.append(copy)

    def join(i):
        view, part, row, count = pieces[i]
        first[i].wait_recv()
        mine = view(core)
        span = pl.ds(row, count)

        @pl.loop(0, 16)
        def _(leaf):
            yy, xx = leaf // 4, leaf % 4
            half[part, yy, xx, span] = mine[yy, xx] + other[part, yy, xx, span]

    def send(part, phase, d, src, dst):
        slot = phase * 3 + d - 1
        copy = pltpu.make_async_remote_copy(
            src_ref=src,
            dst_ref=dst,
            send_sem=send_sem.at[part, slot],
            recv_sem=recv_sem.at[part, slot],
            device_id=device_of(along(at, ORDERS[part][phase], d)),
            device_id_type=MESH,
        )
        copy.start()
        sent.append(copy)
        return copy

    def pick(ref, part, axes, axis, place):
        index = [place if a == axis else slice(None) for a in axes]
        return ref.at[(part, *index)]

    def ship(part, phase, ref, axes, land):
        axis = ORDERS[part][phase]
        return [
            send(part, phase, d, pick(ref, part, axes, axis, lax.rem(at[axis] + d, 4)), land.at[part, d - 1])
            for d in STEPS
        ]

    gp_ref[...] = tn(pooled_ref[...], upstream).reshape(gp_ref.shape)
    swap(0)
    grad_pooled = nt(upstream, proj_ref[...]) * (0.5 / length)

    def spread_back(low):
        for base, titles in ((0, queries), (q_rows, labels)):
            where = pl.ds(0 if titles == queries else queries, titles)
            mine = grad_pooled[:queries] if titles == queries else grad_pooled[queries:]
            mine = mine[:, low : low + channels]

            @pl.loop(0, length)
            def _(p):
                span = pl.ds(pl.multiple_of(base + p * titles, 32), titles)
                grad_pre[span, low : low + channels] = (
                    slope[span, low : low + channels] * mine
                ).astype(bf16)

    waiting = [None] * 3
    spread_back(channels)
    join(0)
    waiting[0] = ship(0, 0, half, "yxz", r1)
    for col in (0, 256):
        part = tn(taps[...], grad_pre[:, channels + col : channels + col + 256])
        g5_ref[:, :, :, :, :, col : col + 256] = part.reshape(g5_ref.shape[:-1] + (256,))
    swap(1)
    swap(2)
    spread_back(0)
    join(1)
    waiting[1] = ship(1, 0, half, "yxz", r1)
    for col in (0, 256):
        part = tn(taps[:, emb : 4 * emb], grad_pre[:, col : col + 256])
        g3_ref[:, :, :, :, :, col : col + 256] = part.reshape(g3_ref.shape[:-1] + (256,))
    swap(3)
    join(2)
    join(3)
    waiting[2] = ship(2, 0, half, "yxz", r1)

    for part in range(3):
        axis = ORDERS[part][0]
        left = "".join(a for a in "yxz" if a != axis)
        wait_all(waiting[part])
        mine = pick(half, part, "yxz", axis, at[axis])

        @pl.loop(0, 4)
        def _(k):
            b[part, k] = (mine[k] + r1[part, 0, k]) + (r1[part, 1, k] + r1[part, 2, k])

        waiting[part] = ship(part, 1, b, left, r2)
    for part in range(3):
        axis = ORDERS[part][1]
        left = "".join(a for a in "yxz" if a not in ORDERS[part][:1])
        wait_all(waiting[part])
        mine = pick(b, part, left, axis, at[axis])
        c[part] = (mine[...] + r2[part, 0]) + (r2[part, 1] + r2[part, 2])
        waiting[part] = ship(part, 2, c, ORDERS[part][2], r3)
    for part in range(3):
        axis = ORDERS[part][2]
        wait_all(waiting[part])
        done[part] = (c[part, at[axis]] + r3[part, 0]) + (r3[part, 1] + r3[part, 2])
    own = pltpu.make_async_copy(done, out_ref.at[core, at["z"]], local_sem)
    own.start()
    final = []
    for i, peer in enumerate(lab_peers):
        copy = pltpu.make_async_remote_copy(
            src_ref=done,
            dst_ref=out_ref.at[core, at["z"]],
            send_sem=out_send.at[i],
            recv_sem=out_recv.at[i],
            device_id=device_of(peer),
            device_id_type=MESH,
        )
        copy.start()
        final.append(copy)
    own.wait()
    for copy in started + sent:
        copy.wait_send()
    for copy in final:
        copy.wait()


def training_window(embedded, three, five, projection, info, own_row, own_col, free_vectors):
    rows, emb = embedded.shape
    channels = three.shape[1]
    nodes, width = free_vectors.shape
    queries, labels = info.shape[0], own_col.shape[0]
    titles = queries + labels
    f32, bf16 = jnp.float32, jnp.bfloat16
    vmem = pl.BlockSpec(memory_space=pltpu.VMEM)
    hbm = pl.BlockSpec(memory_space=pl.ANY)
    dma = pltpu.SemaphoreType.DMA
    loss, grad_free, out = pl.pallas_call(
        window_kernel,
        out_shape=(
            jax.ShapeDtypeStruct((queries, 128), f32),
            jax.ShapeDtypeStruct((nodes, width), f32),
            jax.ShapeDtypeStruct((2, 4, 3, 8, width), f32),
        ),
        in_specs=[vmem, hbm, hbm, hbm, vmem, vmem, vmem, vmem],
        out_specs=(vmem,) * 3,
        scratch_shapes=[
            pltpu.VMEM(three.shape, bf16),
            pltpu.VMEM(five.shape, bf16),
            pltpu.VMEM(projection.shape, bf16),
            pltpu.VMEM((rows, 5 * emb), bf16),
            pltpu.VMEM((rows, 2 * channels), f32),
            pltpu.VMEM((titles, 2 * channels), f32),
            pltpu.VMEM((titles, 2 * channels), bf16),
            pltpu.VMEM((4, 2, 4, 4, queries, width + 128), bf16),
            pltpu.VMEM((4, 2, 4, 4, nodes, width), bf16),
            pltpu.VMEM((nodes, width), f32),
            pltpu.VMEM((queries, width), f32),
            pltpu.VMEM((queries, 256), f32),
            pltpu.VMEM((8, queries, 128), f32),
            pltpu.VMEM((rows, 2 * channels), bf16),
            pltpu.VMEM((4, 4, 2, 4, 8, width), f32),
            pltpu.VMEM((4, 4, 2, 5, 8, width), f32),
            pltpu.VMEM((4, 4, 2, 3, 8, width), f32),
            pltpu.VMEM((3, 4, 4, 4, 8, width), f32),
            pltpu.VMEM((3, 4, 4, 4, 8, width), f32),
            pltpu.VMEM((3, 3, 4, 4, 8, width), f32),
            pltpu.VMEM((3, 4, 4, 8, width), f32),
            pltpu.VMEM((3, 3, 4, 8, width), f32),
            pltpu.VMEM((3, 4, 8, width), f32),
            pltpu.VMEM((3, 3, 8, width), f32),
            pltpu.VMEM((3, 8, width), f32),
            dma((3,)),
            dma((3, 10)),
            dma((3, 10)),
            dma((3, 9)),
            dma((3, 9)),
            dma((2, 12)),
            dma((2, 12)),
            dma((4,)),
            dma((4,)),
            dma((3, 9)),
            dma((3, 9)),
            dma((7,)),
            dma((7,)),
            dma,
        ],
        compiler_params=pltpu.CompilerParams(
            collective_id=1, has_side_effects=True, vmem_limit_bytes=60 << 20
        ),
        name="training_window",
    )(embedded, three, five, projection, info, own_row, own_col, free_vectors)
    by_part = out.transpose(2, 0, 1, 3, 4)
    grad_projection = by_part[0].reshape(64, width)
    grad_five = jnp.concatenate([by_part[1], by_part[2][:, :1]], axis=1).reshape(80, width)
    grad_three = by_part[2][:, 1:].reshape(48, width)
    return loss[:, 0], grad_free, grad_three, grad_five, grad_projection


def per_device(
    query_tokens,
    label_tokens,
    label_node,
    shortlist_owner,
    shortlist_node,
    positives,
    table,
    three,
    five,
    projection,
    free_vectors,
):
    device_index = lax.axis_index("lab") * lax.axis_size("leaf") + lax.axis_index("leaf")
    query_count = query_tokens.shape[0]
    label_count = label_tokens.shape[0]
    node_count = free_vectors.shape[0]

    positive_node = jnp.take(label_node, positives, mode="clip")
    home = positives // label_count * node_count + positive_node
    listed = shortlist_owner[:, :, None] * node_count + shortlist_node
    target = jnp.any(listed[:, :, :, None] == home[:, None, None, :], axis=3)
    codes = (shortlist_node + node_count * target.astype(jnp.int32)).reshape(query_count, -1)
    owners = jnp.broadcast_to(shortlist_owner[:, :, None], shortlist_node.shape).reshape(query_count, -1)
    info = jnp.concatenate([codes, owners], axis=1).astype(jnp.bfloat16)
    own_nodes = lax.dynamic_slice_in_dim(label_node, device_index * label_count, label_count)
    own_row, own_col = own_nodes[None, :], own_nodes[:, None]

    tokens = jnp.concatenate([query_tokens.T.reshape(-1), label_tokens.T.reshape(-1)])
    embedded = jnp.take(table, tokens, axis=0, mode="clip")
    return training_window(
        embedded, three, five, projection, info, own_row, own_col, free_vectors
    )


def solution(mesh):
    both = ("lab", "leaf")
    in_specs = (
        P(both, None),
        P(both, None),
        P(),
        P(both, None),
        P(both, None, None),
        P(both, None),
        P(),
        P(),
        P(),
        P(),
        P(both, None),
    )
    out_specs = (P(both), P(both, None), P("leaf", None), P("leaf", None), P("leaf", None))
    return jax.shard_map(
        per_device, mesh=mesh, in_specs=in_specs, out_specs=out_specs, check_vma=False
    )
```

time: 514 us -> 127 us (0.25)
  waiting for transfers between devices: 366 us -> 0 us
  Pallas kernels: 0 us -> 93.3 us
  matrix products: 44.6 us -> 0 us
  other arithmetic: 30.3 us -> 2.21 us
  blocking collectives: 21.5 us -> 0 us
  between operations: 14.7 us -> 0.75 us
    reduce_scatter x3 -> x0, waiting for transfers between devices: 207 us -> none  [finish(): part = lax.psum_scatter(partial, 'leaf', scatter_dimension=0, tiled=True)]
    all_gather x2 -> x0, waiting for transfers between devices: 96.5 us -> none  [the longest x1 62.8 us: per_device(): all_queries = lax.all_gather(query_rows, axes, axis=0, tiled=True)]
    pallas_call x0 -> x1, Pallas kernels: none -> 93.3 us  [training_window(): pl.pallas_call(window_kernel, out_shape=(jax.ShapeDtypeStruct((queries, 1...]
    psum x1 -> x0, waiting for transfers between devices: 62.4 us -> none  [finish(): return lax.psum(part, 'lab')]
    dot_general x12 -> x0, matrix products: 44.6 us -> none  [the longest x1 11.4 us: per_device(): pre5 = jnp.dot(five_taps, five, preferred_element_type=jnp.float32)]
    all_to_all x1 -> x0, blocking collectives: 21.5 us -> none  [per_device(): lax.all_to_all(code_out, axes, split_axis=0, concat_axis=0, tiled=True)]
    convert_element_type x4 -> x0, other arithmetic: 13.5 us -> none  [the longest x2 12.6 us: back(): return pullback(spread)[0].astype(jnp.bfloat16)]
    reduce_sum x3 -> x0, other arithmetic: 6.99 us -> none  [the longest x2 6.88 us: pool(): jnp.mean(gelu_tanh(v).reshape(length, titles, -1), axis=0)]
  transfers between devices with their start and end apart: 6 -> 0, of which waited for: 6 -> 0; matrix products, arithmetic and copies ran while one was open for 7% -> 0% of each run, Pallas kernels for 0% -> 0%
where the time goes in v2:
time: 127 us
  Pallas kernels  93.3 us (73%)
  local copies, waits for them, and re-layouts  30.5 us (24%)
  other arithmetic  2.21 us (2%)
    pallas_call x1, Pallas kernels, training_window(): pl.pallas_call(window_kernel, out_shape=(jax.ShapeDtypeStruct((queries, 1...  93.3 us
    gather x1, local copies, waits for them, and re-layouts, per_device(): embedded = jnp.take(table, tokens, axis=0, mode='clip')  20.1 us

profile of v2, /device:TPU:1, one launch (start us, length us, event | category | flops | bytes accessed | tf_op | source)
XLA Modules:
  0.0 126.7 jit_solution(7313614060298001172)
XLA Ops:
  0.6 0.0 copy-start
  0.6 1.3 %dynamic-slice_bitcast_fusion = (s32[64,1]{0,1:T(1,128)S(1)}, s32[1,64]{1,0:T(1,128)}) fusion(s32[8192]{0:T(1024)} %param.13, s32[]{:T(128)S(6)} %select_n.9), kind=kLoop, calls=%fused_computation.24 | loop fusion | bytes 772 | tf_op jit(solution)/shard_map/broadcast_in_dim | solution.py:525
  2.0 0.8 broadcast_multiply_fusion
  2.7 0.8 reshape.36
  3.5 0.8 copy.38
  4.3 0.1 reshape.51
  4.4 0.0 copy-done
  4.4 0.0 copy-start.2
  4.4 0.0 copy-start.1
  4.4 1.1 gather_fusion.1
  5.6 0.1 reshape.50
  5.7 0.1 copy.43
  5.8 0.1 copy.45
  5.9 0.0 copy-done.2
  5.9 0.1 copy.37
  6.0 0.1 reshape.35
  6.1 0.0 copy-done.1
  6.1 0.1 copy.44
  6.2 0.7 pad_maximum_fusion.1.info_ref
  6.9 0.7 copy.46.col_ref
  7.6 20.1 %gather_fusion = bf16[3072,256]{1,0:T(8,128)(2,1)} fusion(bf16[32768,256]{1,0:T(8,128)(2,1)} %param.17, s32[3072]{0:T(1024)S(1)} %add_clamp_fusion), kind=kCustom, calls=%fused_computation | custom fusion | bytes 3158016 | tf_op jit(solution)/shard_map/jit(_take)/gather | solution.py:528
  27.7 93.3 %training_window.1 = (f32[32,128]{1,0:T(8,128)}, f32[16,512]{1,0:T(8,128)}, f32[2,4,3,8,512]{4,3,2,1,0:T(8,128)}) custom-call(bf16[3072,256]{1,0:T(8,128)(2,1)} %gather_fusion, bf16[768,512]{1,0:T(8,128)(2,1)} %w3_hbm.1, bf16[1280,512]{1,0:T(8,128)(2,1)} %w5_hbm.1, bf16[1024,512]{1,0:T(8,128)(2,1)} %proj_hbm.1, bf16[32,128]{1,0:T(8,128)(2,1)} %pad_maximum_fusion.1.info_ref, ...), custom_call_target="tpu_custom_call" | custom-call | tf_op jit(solution)/shard_map/training_window/pallas_call | solution.py:437
  121.0 1.3 %slice_reduce_fusion = f32[32]{0:T(128)} fusion(f32[32,128]{1,0:T(8,128)} %get-tuple-element.8), kind=kLoop, calls=%fused_computation.15 | loop fusion | bytes 256 | tf_op jit(solution)/shard_map/slice | solution.py:496
  122.3 1.7 %fusion.5 = (f32[1,2,4,8,512]{4,3,0,2,1:T(8,128)}, f32[2,4,8,512]{3,2,1,0:T(8,128)S(1)}, f32[2,4,8,512]{3,2,1,0:T(8,128)S(1)}) fusion(f32[3,2,4,8,512]{4,3,0,2,1:T(8,128)} %bitcast.20), kind=kLoop, calls=%fused_computation.26 | loop fusion | bytes 786432 | tf_op jit(solution)/shard_map/slice | solution.py:493
  124.0 0.6 slice.30
  124.7 0.7 pad_maximum_fusion
  125.4 1.4 %copy.50 = f32[16,512]{1,0:T(8,128)} copy(f32[16,512]{1,0:T(8,128)} %get-tuple-element.24) | data formatting | bytes 65536
  (8 shorter events, 0.1 us)
Async XLA Ops:
  0.6 3.8 %copy-start = (s32[8192]{0:T(1024)S(1)}, s32[8192]{0:T(1024)}, u32[]{:S(2)}) copy-start(s32[8192]{0:T(1024)} %param.13) | copy-start | bytes 98308
  4.4 1.5 %copy-start.2 = (s32[32,32]{1,0:T(8,128)S(1)}, s32[32,32]{1,0:T(8,128)}, u32[]{:S(2)}) copy-start(s32[32,32]{1,0:T(8,128)} %param.11) | copy-start | bytes 12292
  4.4 1.6 %copy-start.1 = (s32[32,8,8]{0,2,1:T(8,128)S(1)}, s32[32,8,8]{0,2,1:T(8,128)}, u32[]{:S(2)}) copy-start(s32[32,8,8]{0,2,1:T(8,128)} %param.15) | copy-start | bytes 24580

commit v3 on v2

--- a/solution.py
+++ b/solution.py
@@ -31,17 +31,48 @@
 Q_PARTS = ((0, 256), (256, 256), (512, 128))
 H_PARTS = ((0, 128), (128, 128), (256, 256))
 STEPS = (1, 3, 2)
+WAVE_UNITS = (((0, 1), (1, 1), (2, 2)), ((0, 2), (2, 2), (4, 1)), ((0, 1), (1, 1), (2, 1)))
+
+
+def shortlist_codes(nodes_ref, listed_ref, owner_ref, positive_ref, nodes, labels):
+    bf16, f32 = jnp.bfloat16, jnp.float32
+    count, queries = listed_ref.shape
+    each = count // owner_ref.shape[0]
+    listed = listed_ref[...]
+    owners = jnp.concatenate(
+        [jnp.broadcast_to(owner_ref[k : k + 1, :], (each, queries)) for k in range(count // each)], axis=0
+    )
+    table = nodes_ref[...].astype(f32).astype(bf16)
+    lanes = table.shape[1]
+    hit = jnp.zeros((count, queries), f32)
+    for j in range(positive_ref.shape[0]):
+        label = positive_ref[j : j + 1, :]
+        row = lax.broadcasted_iota(jnp.int32, (table.shape[0], queries), 0) == label // lanes
+        column = lax.broadcasted_iota(jnp.int32, (lanes, queries), 0) == label % lanes
+        found = lax.dot_general(
+            table, jnp.where(row, 1.0, 0.0).astype(bf16), (((0,), (0,)), ((), ())),
+            preferred_element_type=f32,
+        )
+        node = jnp.sum(jnp.where(column, found, 0.0), axis=0, keepdims=True)
+        same = (owners == label // labels) & (listed.astype(f32) == node)
+        hit = jnp.where(same, 1.0, hit)
+    codes = jnp.concatenate([listed.astype(f32) + nodes * hit, owners.astype(f32)], axis=0)
+    square = (queries, queries)
+    eye = lax.broadcasted_iota(jnp.int32, square, 0) == lax.broadcasted_iota(jnp.int32, square, 1)
+    return lax.dot_general(
+        jnp.where(eye, 1.0, 0.0).astype(bf16), codes.astype(bf16), (((1,), (1,)), ((), ())),
+        preferred_element_type=f32,
+    )
 
 
 def window_kernel(
-    emb_ref, w3_hbm, w5_hbm, proj_hbm, info_ref, row_ref, col_ref, free_vec_ref,
-    loss_ref, free_ref, out_ref,
+    emb_ref, w3_hbm, w5_hbm, proj_hbm, nodes_ref, listed_ref, owner_ref, positive_ref, free_vec_ref,
+    loss_ref, free_ref, out3_ref, out5_ref, outp_ref,
     w3_ref, w5_ref, proj_ref, taps, slope, total, pooled_ref,
     all_q, all_h, free_acc, grad_acc, loss_acc, tiles,
-    grad_pre, gp_ref, g5_ref, g3_ref,
-    half, other, r1, b, r2, c, r3, done,
+    grad_pre, waves,
     load_sem, q_send, q_recv, h_send, h_recv, over_send, over_recv,
-    core_send, core_recv, send_sem, recv_sem, out_send, out_recv, local_sem,
+    core_send, core_recv, send_sem, recv_sem, out_send, out_recv,
 ):
     at = where_am_i()
     bf16, f32 = jnp.bfloat16, jnp.float32
@@ -50,8 +81,7 @@
     lab_steps = [(z, cc) for z in range(4) for cc in range(2)][1:]
     lab_peers = [along(along(at, "z", z), "c", cc) for z, cc in lab_steps]
     home = (at["z"], at["c"], at["y"], at["x"])
-    queries = info_ref.shape[0]
-    labels = col_ref.shape[0]
+    queries, labels = listed_ref.shape[1], 64
     nodes, width = free_vec_ref.shape
     rows, emb = emb_ref.shape
     length = rows // (queries + labels)
@@ -161,8 +191,9 @@
     convolve(512, queries, False)
     unfold(q_rows, labels)
     loads[2].wait()
+    info = shortlist_codes(nodes_ref, listed_ref, owner_ref, positive_ref, nodes, labels)
     all_q[(*home, slice(None), pl.ds(0, width))] = encoded_of(pl.ds(0, queries)).astype(bf16)
-    all_q[(*home, slice(None), pl.ds(width, wide - width))] = info_ref[...]
+    all_q[(*home, slice(None), pl.ds(width, wide - width))] = info.astype(bf16)
     pl.semaphore_wait(barrier, len(peers))
     q_stage = [direct(all_q, Q_PARTS, q_send, q_recv, part, 0) for part in range(3)]
     over = []
@@ -184,7 +215,10 @@
     convolve(q_rows + 1024, labels, False)
     convolve(q_rows + 1536, labels, False)
     label_encoded = encoded_of(pl.ds(queries, labels))
-    member = lax.broadcasted_iota(jnp.int32, (nodes, labels), 0) == row_ref[...]
+    index = at["z"] * 32 + at["c"] * 16 + at["y"] * 4 + at["x"]
+    pair = jnp.broadcast_to(nodes_ref[pl.ds(index // 2, 1), :].astype(f32), (nodes, 2 * labels))
+    pair = jnp.where(lax.rem(index, 2) == 0, pair, pltpu.roll(pair, labels, 1))[:, :labels]
+    member = lax.broadcasted_iota(jnp.int32, (nodes, labels), 0).astype(f32) == pair
     member = jnp.where(member, 1.0, 0.0)
     counts = jnp.sum(member, axis=1, keepdims=True)
     sums = jnp.dot(member, label_encoded, precision=lax.Precision.HIGHEST, preferred_element_type=f32)
@@ -205,7 +239,6 @@
         wait_all(h_stage[part])
         h_stage[part] = direct(all_h, H_PARTS, h_send, h_recv, part, 1)
 
-    info = info_ref[...].astype(f32)
     lane = lax.rem(lax.broadcasted_iota(jnp.int32, (queries, 128), 1), nodes).astype(f32)
     for k in range(8):
         tile = jnp.zeros((queries, 128), f32)
@@ -224,7 +257,7 @@
         h_over.append(hand_over(all_h, H_PARTS, 1, part, 0))
     wait_all(over)
 
-    me = ((at["z"] * 2 + at["c"]) * 16 + at["y"] * 4 + at["x"]).astype(f32)
+    me = index.astype(f32)
     fold_row = lax.broadcasted_iota(jnp.int32, (8, 128), 0)
     fold_col = lax.broadcasted_iota(jnp.int32, (8, 128), 1)
     fold = jnp.where((lax.rem(fold_col, 8) == fold_row) & (fold_col < 64), 1.0, 0.0).astype(bf16)
@@ -278,74 +311,126 @@
         weight = (SCORE_SCALE * (jax.nn.sigmoid(scores) - target) * live).astype(bf16)
         grad_acc[...] += jnp.dot(weight, keys, preferred_element_type=f32)
 
-    loss_ref[...] = jnp.broadcast_to(jnp.sum(loss_acc[...], axis=1, keepdims=True), loss_ref.shape)
+    loss = jnp.sum(loss_acc[...], axis=1, keepdims=True)
+    same = (queries, queries)
+    eye = lax.broadcasted_iota(jnp.int32, same, 0) == lax.broadcasted_iota(jnp.int32, same, 1)
+    loss_ref[...] = jnp.sum(jnp.where(eye, loss, 0.0), axis=0, keepdims=True)
     free = free_acc[...]
     free_ref[...] = free
-    spread = jnp.where(lax.broadcasted_iota(jnp.int32, (labels, nodes), 1) == col_ref[...], 1.0, 0.0)
-    label_up = jnp.dot(spread.astype(bf16), (free / counts).astype(bf16), preferred_element_type=f32)
+    label_up = tn(member.astype(bf16), (free / counts).astype(bf16))
     upstream = jnp.concatenate([grad_acc[...].astype(bf16), label_up.astype(bf16)], axis=0)
 
     sent = []
-    first = {}
-    pieces = (
-        (lambda k: gp_ref.at[:, :, k], 0, 0, 4),
-        (lambda k: g5_ref.at[:, :, k, pl.ds(0, 4)], 1, 0, 4),
-        (lambda k: g5_ref.at[:, :, k, pl.ds(4, 1)], 2, 0, 1),
-        (lambda k: g3_ref.at[:, :, k], 2, 1, 3),
-    )
-
-    def swap(i):
-        view, part, row, count = pieces[i]
-        copy = pltpu.make_async_remote_copy(
-            src_ref=view(1 - core),
-            dst_ref=other.at[part, :, :, pl.ds(row, count)],
-            send_sem=core_send.at[i],
-            recv_sem=core_recv.at[i],
+    lane_of = lambda place: pl.ds(pl.multiple_of(128 * place, 128), 128)
+
+    def ship(wave, part, phase, view, land):
+        axis = ORDERS[part][phase]
+        copies = []
+        for d in STEPS:
+            slot = phase * 3 + d - 1
+            copy = pltpu.make_async_remote_copy(
+                src_ref=view(lax.rem(at[axis] + d, 4)),
+                dst_ref=land.at[d - 1],
+                send_sem=send_sem.at[wave * 3 + part, slot],
+                recv_sem=recv_sem.at[wave * 3 + part, slot],
+                device_id=device_of(along(at, axis, d)),
+                device_id_type=MESH,
+            )
+            copy.start()
+            copies.append(copy)
+        sent.extend(copies)
+        return copies
+
+    def add(target, mine, land, steps):
+        @pl.loop(0, steps)
+        def _(k):
+            target[k] = (mine(k) + land[0, k]) + (land[1, k] + land[2, k])
+
+    def reduce_wave(wave, out_ref):
+        own, other, done, parts = waves[wave]
+        swap = pltpu.make_async_remote_copy(
+            src_ref=own.at[:, :, 1 - core],
+            dst_ref=other,
+            send_sem=core_send.at[wave],
+            recv_sem=core_recv.at[wave],
             device_id=device_of(partner),
             device_id_type=MESH,
         )
-        copy.start()
-        first[i] = copy
-        sent.append(copy)
-
-    def join(i):
-        view, part, row, count = pieces[i]
-        first[i].wait_recv()
-        mine = view(core)
-        span = pl.ds(row, count)
+        swap.start()
+        sent.append(swap)
+        yield
+        swap.wait_recv()
 
         @pl.loop(0, 16)
         def _(leaf):
             yy, xx = leaf // 4, leaf % 4
-            half[part, yy, xx, span] = mine[yy, xx] + other[part, yy, xx, span]
-
-    def send(part, phase, d, src, dst):
-        slot = phase * 3 + d - 1
-        copy = pltpu.make_async_remote_copy(
-            src_ref=src,
-            dst_ref=dst,
-            send_sem=send_sem.at[part, slot],
-            recv_sem=recv_sem.at[part, slot],
-            device_id=device_of(along(at, ORDERS[part][phase], d)),
-            device_id_type=MESH,
-        )
-        copy.start()
-        sent.append(copy)
-        return copy
-
-    def pick(ref, part, axes, axis, place):
-        index = [place if a == axis else slice(None) for a in axes]
-        return ref.at[(part, *index)]
-
-    def ship(part, phase, ref, axes, land):
-        axis = ORDERS[part][phase]
-        return [
-            send(part, phase, d, pick(ref, part, axes, axis, lax.rem(at[axis] + d, 4)), land.at[part, d - 1])
-            for d in STEPS
+            own[yy, xx, core] += other[yy, xx]
+
+        x, y, z = at["x"], at["y"], at["z"]
+        us = [pl.ds(*units) for units in WAVE_UNITS[wave]]
+        mine = own.at[:, :, core]
+        (r1x, bx, r2x, cx, r3x), (r1y, by, r2y, cy, r3y), (r1z, bz, r2z, cz, r3z) = parts
+        waiting = [
+            ship(wave, 0, 0, lambda p: own.at[:, p, core, us[0]], r1x),
+            ship(wave, 1, 0, lambda p: own.at[p, :, core, us[1]], r1y),
+            ship(wave, 2, 0, lambda p: own.at[:, :, core, us[2], :, lane_of(p)], r1z),
         ]
-
+        yield
+        wait_all(waiting[0])
+        add(bx, lambda k: own[k, x, core, us[0]], r1x, 4)
+        waiting[0] = ship(wave, 0, 1, lambda p: bx.at[p], r2x)
+        wait_all(waiting[1])
+        add(by, lambda k: own[y, k, core, us[1]], r1y, 4)
+        waiting[1] = ship(wave, 1, 1, lambda p: by.at[:, :, :, lane_of(p)], r2y)
+        wait_all(waiting[2])
+        for xx in range(4):
+
+            @pl.loop(0, 4)
+            def _(k, xx=xx):
+                first = own[k, xx, core, us[2], :, lane_of(z)]
+                bz[k, xx] = (first + r1z[0, k, xx]) + (r1z[1, k, xx] + r1z[2, k, xx])
+
+        waiting[2] = ship(wave, 2, 1, lambda p: bz.at[:, p], r2z)
+        yield
+        wait_all(waiting[0])
+        cx[...] = (bx[y] + r2x[0]) + (r2x[1] + r2x[2])
+        waiting[0] = ship(wave, 0, 2, lambda p: cx.at[:, :, lane_of(p)], r3x)
+        wait_all(waiting[1])
+        add(cy, lambda k: by[k, :, :, lane_of(z)], r2y, 4)
+        waiting[1] = ship(wave, 1, 2, lambda p: cy.at[p], r3y)
+        wait_all(waiting[2])
+        add(cz, lambda k: bz[k, x], r2z, 4)
+        waiting[2] = ship(wave, 2, 2, lambda p: cz.at[p], r3z)
+        yield
+        wait_all(waiting[0])
+        done[us[0]] = (cx[:, :, lane_of(z)] + r3x[0]) + (r3x[1] + r3x[2])
+        wait_all(waiting[1])
+        done[us[1]] = (cy[x] + r3y[0]) + (r3y[1] + r3y[2])
+        wait_all(waiting[2])
+        done[us[2]] = (cz[y] + r3z[0]) + (r3z[1] + r3z[2])
+        place = out_ref.at[core, :, :, lane_of(z)]
+        final = []
+        for i, peer in enumerate(lab_peers):
+            copy = pltpu.make_async_remote_copy(
+                src_ref=done,
+                dst_ref=place,
+                send_sem=out_send.at[wave, i],
+                recv_sem=out_recv.at[wave, i],
+                device_id=device_of(peer),
+                device_id_type=MESH,
+            )
+            copy.start()
+            final.append(copy)
+        out_ref[core, :, :, lane_of(z)] = done[...]
+        yield
+        for copy in final:
+            copy.wait()
+        yield
+
+    gp_ref, g5_ref, g3_ref = (waves[i][0] for i in range(3))
     gp_ref[...] = tn(pooled_ref[...], upstream).reshape(gp_ref.shape)
-    swap(0)
+    move_p = reduce_wave(0, outp_ref)
+    next(move_p)
     grad_pooled = nt(upstream, proj_ref[...]) * (0.5 / length)
 
     def spread_back(low):
@@ -361,88 +446,88 @@
                     slope[span, low : low + channels] * mine
                 ).astype(bf16)
 
-    waiting = [None] * 3
+    def weigh(ref, left, low):
+        right = grad_pre[:, low : low + 256]
+        col = low % channels
+        ref[:, :, :, :, :, col : col + 256] = tn(left(), right).reshape(ref.shape[:-1] + (256,))
+
     spread_back(channels)
-    join(0)
-    waiting[0] = ship(0, 0, half, "yxz", r1)
-    for col in (0, 256):
-        part = tn(taps[...], grad_pre[:, channels + col : channels + col + 256])
-        g5_ref[:, :, :, :, :, col : col + 256] = part.reshape(g5_ref.shape[:-1] + (256,))
-    swap(1)
-    swap(2)
+    next(move_p)
+    weigh(g5_ref, lambda: taps[...], channels)
+    weigh(g5_ref, lambda: taps[...], channels + 256)
+    move_5 = reduce_wave(1, out5_ref)
+    next(move_5)
+    next(move_p)
     spread_back(0)
-    join(1)
-    waiting[1] = ship(1, 0, half, "yxz", r1)
-    for col in (0, 256):
-        part = tn(taps[:, emb : 4 * emb], grad_pre[:, col : col + 256])
-        g3_ref[:, :, :, :, :, col : col + 256] = part.reshape(g3_ref.shape[:-1] + (256,))
-    swap(3)
-    join(2)
-    join(3)
-    waiting[2] = ship(2, 0, half, "yxz", r1)
-
-    for part in range(3):
-        axis = ORDERS[part][0]
-        left = "".join(a for a in "yxz" if a != axis)
-        wait_all(waiting[part])
-        mine = pick(half, part, "yxz", axis, at[axis])
-
-        @pl.loop(0, 4)
-        def _(k):
-            b[part, k] = (mine[k] + r1[part, 0, k]) + (r1[part, 1, k] + r1[part, 2, k])
-
-        waiting[part] = ship(part, 1, b, left, r2)
-    for part in range(3):
-        axis = ORDERS[part][1]
-        left = "".join(a for a in "yxz" if a not in ORDERS[part][:1])
-        wait_all(waiting[part])
-        mine = pick(b, part, left, axis, at[axis])
-        c[part] = (mine[...] + r2[part, 0]) + (r2[part, 1] + r2[part, 2])
-        waiting[part] = ship(part, 2, c, ORDERS[part][2], r3)
-    for part in range(3):
-        axis = ORDERS[part][2]
-        wait_all(waiting[part])
-        done[part] = (c[part, at[axis]] + r3[part, 0]) + (r3[part, 1] + r3[part, 2])
-    own = pltpu.make_async_copy(done, out_ref.at[core, at["z"]], local_sem)
-    own.start()
-    final = []
-    for i, peer in enumerate(lab_peers):
-        copy = pltpu.make_async_remote_copy(
-            src_ref=done,
-            dst_ref=out_ref.at[core, at["z"]],
-            send_sem=out_send.at[i],
-            recv_sem=out_recv.at[i],
-            device_id=device_of(peer),
-            device_id_type=MESH,
-        )
-        copy.start()
-        final.append(copy)
-    own.wait()
+    next(move_5)
+    weigh(g3_ref, lambda: taps[:, emb : 4 * emb], 0)
+    next(move_p)
+    weigh(g3_ref, lambda: taps[:, emb : 4 * emb], 256)
+    move_3 = reduce_wave(2, out3_ref)
+    next(move_3)
+    next(move_p)
+    next(move_5)
+    next(move_3)
+    next(move_5)
+    next(move_3)
+    next(move_5)
+    next(move_3)
+    next(move_3)
+    for move in (move_p, move_5, move_3):
+        next(move)
     for copy in started + sent:
         copy.wait_send()
-    for copy in final:
-        copy.wait()
-
-
-def training_window(embedded, three, five, projection, info, own_row, own_col, free_vectors):
+
+
+def copy_out_kernel(*refs):
+    for source, target in zip(refs[: len(refs) // 2], refs[len(refs) // 2 :]):
+        target[...] = source[...]
+
+
+def wave_scratch(units, width):
+    f32 = jnp.float32
+    count = sum(n for _, n in units)
+    nx, ny, nz = (n for _, n in units)
+
+    def pads(*shapes):
+        return [pltpu.VMEM(shape, f32) for shape in shapes]
+
+    return [
+        pltpu.VMEM((4, 4, 2, count, 8, width), f32),
+        pltpu.VMEM((4, 4, count, 8, width), f32),
+        pltpu.VMEM((count, 8, 128), f32),
+        [
+            pads((3, 4, nx, 8, width), (4, nx, 8, width), (3, nx, 8, width), (nx, 8, width), (3, nx, 8, 128)),
+            pads((3, 4, ny, 8, width), (4, ny, 8, width), (3, 4, ny, 8, 128), (4, ny, 8, 128), (3, ny, 8, 128)),
+            pads(
+                (3, 4, 4, nz, 8, 128), (4, 4, nz, 8, 128), (3, 4, nz, 8, 128), (4, nz, 8, 128), (3, nz, 8, 128)
+            ),
+        ],
+    ]
+
+
+def training_window(embedded, three, five, projection, label_node, listed, owner, positives, free_vectors):
     rows, emb = embedded.shape
     channels = three.shape[1]
     nodes, width = free_vectors.shape
-    queries, labels = info.shape[0], own_col.shape[0]
-    titles = queries + labels
+    queries = listed.shape[1]
+    titles = queries + 64
     f32, bf16 = jnp.float32, jnp.bfloat16
     vmem = pl.BlockSpec(memory_space=pltpu.VMEM)
     hbm = pl.BlockSpec(memory_space=pl.ANY)
     dma = pltpu.SemaphoreType.DMA
-    loss, grad_free, out = pl.pallas_call(
+    shapes = (
+        jax.ShapeDtypeStruct((1, queries), f32),
+        jax.ShapeDtypeStruct((nodes, width), f32),
+        jax.ShapeDtypeStruct((2, 3, 8, width), f32),
+        jax.ShapeDtypeStruct((2, 5, 8, width), f32),
+        jax.ShapeDtypeStruct((2, 4, 8, width), f32),
+    )
+    outs = pl.pallas_call(
         window_kernel,
-        out_shape=(
-            jax.ShapeDtypeStruct((queries, 128), f32),
-            jax.ShapeDtypeStruct((nodes, width), f32),
-            jax.ShapeDtypeStruct((2, 4, 3, 8, width), f32),
-        ),
-        in_specs=[vmem, hbm, hbm, hbm, vmem, vmem, vmem, vmem],
-        out_specs=(vmem,) * 3,
+        out_shape=shapes,
+        in_specs=[vmem, hbm, hbm, hbm, vmem, vmem, vmem, vmem, vmem],
+        out_specs=(vmem,) * 5,
         scratch_shapes=[
             pltpu.VMEM(three.shape, bf16),
             pltpu.VMEM(five.shape, bf16),
@@ -458,17 +543,7 @@
             pltpu.VMEM((queries, 256), f32),
             pltpu.VMEM((8, queries, 128), f32),
             pltpu.VMEM((rows, 2 * channels), bf16),
-            pltpu.VMEM((4, 4, 2, 4, 8, width), f32),
-            pltpu.VMEM((4, 4, 2, 5, 8, width), f32),
-            pltpu.VMEM((4, 4, 2, 3, 8, width), f32),
-            pltpu.VMEM((3, 4, 4, 4, 8, width), f32),
-            pltpu.VMEM((3, 4, 4, 4, 8, width), f32),
-            pltpu.VMEM((3, 3, 4, 4, 8, width), f32),
-            pltpu.VMEM((3, 4, 4, 8, width), f32),
-            pltpu.VMEM((3, 3, 4, 8, width), f32),
-            pltpu.VMEM((3, 4, 8, width), f32),
-            pltpu.VMEM((3, 3, 8, width), f32),
-            pltpu.VMEM((3, 8, width), f32),
+            [wave_scratch(units, width) for units in WAVE_UNITS],
             dma((3,)),
             dma((3, 10)),
             dma((3, 10)),
@@ -476,24 +551,32 @@
             dma((3, 9)),
             dma((2, 12)),
             dma((2, 12)),
-            dma((4,)),
-            dma((4,)),
-            dma((3, 9)),
-            dma((3, 9)),
-            dma((7,)),
-            dma((7,)),
-            dma,
+            dma((3,)),
+            dma((3,)),
+            dma((9, 9)),
+            dma((9, 9)),
+            dma((3, 7)),
+            dma((3, 7)),
         ],
         compiler_params=pltpu.CompilerParams(
             collective_id=1, has_side_effects=True, vmem_limit_bytes=60 << 20
         ),
         name="training_window",
-    )(embedded, three, five, projection, info, own_row, own_col, free_vectors)
-    by_part = out.transpose(2, 0, 1, 3, 4)
-    grad_projection = by_part[0].reshape(64, width)
-    grad_five = jnp.concatenate([by_part[1], by_part[2][:, :1]], axis=1).reshape(80, width)
-    grad_three = by_part[2][:, 1:].reshape(48, width)
-    return loss[:, 0], grad_free, grad_three, grad_five, grad_projection
+    )(embedded, three, five, projection, label_node, listed, owner, positives, free_vectors)
+    loss, grad_free, grad_three, grad_five, grad_projection = pl.pallas_call(
+        copy_out_kernel,
+        out_shape=shapes,
+        in_specs=[vmem] * 5,
+        out_specs=(vmem,) * 5,
+        name="copy_out",
+    )(*outs)
+    return (
+        loss.reshape(queries),
+        grad_free,
+        grad_three.reshape(48, width),
+        grad_five.reshape(80, width),
+        grad_projection.reshape(64, width),
+    )
 
 
 def per_device(
@@ -509,25 +592,18 @@
     projection,
     free_vectors,
 ):
-    device_index = lax.axis_index("lab") * lax.axis_size("leaf") + lax.axis_index("leaf")
-    query_count = query_tokens.shape[0]
-    label_count = label_tokens.shape[0]
-    node_count = free_vectors.shape[0]
-
-    positive_node = jnp.take(label_node, positives, mode="clip")
-    home = positives // label_count * node_count + positive_node
-    listed = shortlist_owner[:, :, None] * node_count + shortlist_node
-    target = jnp.any(listed[:, :, :, None] == home[:, None, None, :], axis=3)
-    codes = (shortlist_node + node_count * target.astype(jnp.int32)).reshape(query_count, -1)
-    owners = jnp.broadcast_to(shortlist_owner[:, :, None], shortlist_node.shape).reshape(query_count, -1)
-    info = jnp.concatenate([codes, owners], axis=1).astype(jnp.bfloat16)
-    own_nodes = lax.dynamic_slice_in_dim(label_node, device_index * label_count, label_count)
-    own_row, own_col = own_nodes[None, :], own_nodes[:, None]
-
     tokens = jnp.concatenate([query_tokens.T.reshape(-1), label_tokens.T.reshape(-1)])
     embedded = jnp.take(table, tokens, axis=0, mode="clip")
     return training_window(
-        embedded, three, five, projection, info, own_row, own_col, free_vectors
+        embedded,
+        three,
+        five,
+        projection,
+        label_node.reshape(-1, 128),
+        shortlist_node.transpose(1, 2, 0).reshape(-1, query_tokens.shape[0]),
+        shortlist_owner.T,
+        positives.T,
+        free_vectors,
     )
 
 

time: 127 us -> 117 us (0.921)
  local copies, waits for them, and re-layouts: 30.5 us -> 21.9 us
  other arithmetic: 2.21 us -> 0.01 us
    slice x4 -> x0, local copies, waits for them, and re-layouts: 3.71 us -> none  [the longest x1 1.72 us: training_window(): grad_projection = by_part[0].reshape(64, width)]
    unnamed x8 -> x0, local copies, waits for them, and re-layouts: 2.16 us -> none
    broadcast_in_dim x3 -> x0, local copies, waits for them, and re-layouts: 2.14 us -> none  [the longest x2 2.04 us: per_device(): own_row, own_col = (own_nodes[None, :], own_nodes[:, None])]
    concatenate x2 -> x0, other arithmetic: 1.37 us -> none  [the longest x1 0.69 us: per_device(): info = jnp.concatenate([codes, owners], axis=1).astype(jnp.bfloat16)]
    pallas_call x1 -> x2, Pallas kernels: 93.3 us -> 93.7 us  [the longest x1 91.9 us: training_window(): pl.pallas_call(window_kernel, out_shape=shapes, in_specs=[vmem, hbm, hbm,...]
where the time goes in v3:
time: 117 us; the launch traced here: 116 us
  Pallas kernels  93.7 us (80%)
  local copies, waits for them, and re-layouts  21.9 us (19%)
    pallas_call x1, Pallas kernels, training_window(): pl.pallas_call(window_kernel, out_shape=shapes, in_specs=[vmem, hbm, hbm,...  91.9 us
    gather x1, local copies, waits for them, and re-layouts, per_device(): embedded = jnp.take(table, tokens, axis=0, mode='clip')  20.3 us

profile of v3, /device:TPU:1, one launch (start us, length us, event | category | flops | bytes accessed | tf_op | source)
XLA Modules:
  0.0 116.2 jit_solution(17152907355749571667)
XLA Ops:
  0.6 0.8 reshape.35
  1.4 0.8 copy.16
  2.2 0.1 reshape.34
  2.3 20.3 %gather_fusion = bf16[3072,256]{1,0:T(8,128)(2,1)} fusion(bf16[32768,256]{1,0:T(8,128)(2,1)} %param.17, s32[3072]{0:T(1024)S(1)} %add_clamp_fusion), kind=kCustom, calls=%fused_computation | custom fusion | bytes 3158016 | tf_op jit(solution)/shard_map/jit(_take)/gather | solution.py:596
  22.5 91.9 %training_window.1 = (f32[1,32]{1,0:T(1,128)}, f32[16,512]{1,0:T(8,128)}, f32[2,3,8,512]{3,2,1,0:T(8,128)}, f32[2,5,8,512]{3,2,1,0:T(8,128)}, f32[2,4,8,512]{3,2,1,0:T(8,128)}) custom-call(bf16[3072,256]{1,0:T(8,128)(2,1)} %gather_fusion, bf16[768,512]{1,0:T(8,128)(2,1)} %w3_hbm.1, bf16[1280,512]{1,0:T(8,128)(2,1)} %w5_hbm.1, bf16[1024,512]{1,0:T(8,128)(2,1)} %proj_hbm.1, ...), custom_call_target="tpu_custom_call" | custom-call | tf_op jit(solution)/shard_map/training_window/pallas_call | solution.py:526
  114.4 1.8 %copy_out.1 = (f32[1,32]{1,0:T(1,128)}, f32[16,512]{1,0:T(8,128)}, f32[2,3,8,512]{3,2,1,0:T(8,128)}, f32[2,5,8,512]{3,2,1,0:T(8,128)}, f32[2,4,8,512]{3,2,1,0:T(8,128)}) custom-call(f32[1,32]{1,0:T(1,128)} %get-tuple-element.15.refs_0_, f32[16,512]{1,0:T(8,128)} %get-tuple-element.16.refs_1_, f32[2,3,8,512]{3,2,1,0:T(8,128)} %get-tuple-element.17.refs_2_, ...), custom_call_target="tpu_custom_call" | custom-call | tf_op jit(solution)/shard_map/copy_out/pallas_call | solution.py:566
  (1 shorter events, 0.0 us)

commit v4 on v3

--- a/solution.py
+++ b/solution.py
@@ -247,14 +247,14 @@
             tile += jnp.where(code == lane, 1.0, 0.0) + jnp.where(code == lane + nodes, 2.0, 0.0)
         tiles[k] = tile
 
-    for part in range(3):
-        wait_all(far[2 * part : 2 * part + 2])
-        over.append(hand_over(all_q, Q_PARTS, 0, part, 2))
     h_over = []
     for part in range(3):
         wait_all(h_stage[part])
         h_stage[part] = direct(all_h, H_PARTS, h_send, h_recv, part, 2)
         h_over.append(hand_over(all_h, H_PARTS, 1, part, 0))
+    for part in range(3):
+        wait_all(far[2 * part : 2 * part + 2])
+        over.append(hand_over(all_q, Q_PARTS, 0, part, 2))
     wait_all(over)
 
     me = index.astype(f32)
@@ -266,7 +266,7 @@
     loss_acc[...] = jnp.zeros_like(loss_acc)
     node = lax.broadcasted_iota(jnp.int32, (nodes, 512), 0).astype(f32) + 1.0
 
-    @pl.loop(0, 8)
+    @pl.loop(0, 8, unroll=4)
     def _(i):
         chunk = all_q[i // 2, i % 2].reshape(512, wide)
         keys = chunk[:, :width]
@@ -293,7 +293,7 @@
 
     own_rows = all_q[(*home, slice(None), pl.ds(0, width))]
 
-    @pl.loop(0, 8)
+    @pl.loop(0, 8, unroll=4)
     def _(i):
         keys = all_h[i // 2, i % 2].reshape(256, width)
         scores = SCORE_SCALE * nt(own_rows, keys)
@@ -342,33 +342,33 @@
         return copies
 
     def add(target, mine, land, steps):
-        @pl.loop(0, steps)
-        def _(k):
+        for k in range(steps):
             target[k] = (mine(k) + land[0, k]) + (land[1, k] + land[2, k])
 
     def reduce_wave(wave, out_ref):
         own, other, done, parts = waves[wave]
-        swap = pltpu.make_async_remote_copy(
-            src_ref=own.at[:, :, 1 - core],
-            dst_ref=other,
-            send_sem=core_send.at[wave],
-            recv_sem=core_recv.at[wave],
-            device_id=device_of(partner),
-            device_id_type=MESH,
-        )
-        swap.start()
-        sent.append(swap)
-        yield
-        swap.wait_recv()
-
-        @pl.loop(0, 16)
-        def _(leaf):
-            yy, xx = leaf // 4, leaf % 4
-            own[yy, xx, core] += other[yy, xx]
+        swaps = []
+        for i in range(2):
+            columns = pl.ds(256 * i, 256)
+            swap = pltpu.make_async_remote_copy(
+                src_ref=own.at[:, :, 1 - core, :, :, columns],
+                dst_ref=other.at[:, :, :, :, columns],
+                send_sem=core_send.at[wave, i],
+                recv_sem=core_recv.at[wave, i],
+                device_id=device_of(partner),
+                device_id_type=MESH,
+            )
+            swap.start()
+            swaps.append(swap)
+            yield
+        sent.extend(swaps)
+        wait_all(swaps)
+        for yy in range(4):
+            for xx in range(4):
+                own[yy, xx, core] += other[yy, xx]
 
         x, y, z = at["x"], at["y"], at["z"]
         us = [pl.ds(*units) for units in WAVE_UNITS[wave]]
-        mine = own.at[:, :, core]
         (r1x, bx, r2x, cx, r3x), (r1y, by, r2y, cy, r3y), (r1z, bz, r2z, cz, r3z) = parts
         waiting = [
             ship(wave, 0, 0, lambda p: own.at[:, p, core, us[0]], r1x),
@@ -384,9 +384,7 @@
         waiting[1] = ship(wave, 1, 1, lambda p: by.at[:, :, :, lane_of(p)], r2y)
         wait_all(waiting[2])
         for xx in range(4):
-
-            @pl.loop(0, 4)
-            def _(k, xx=xx):
+            for k in range(4):
                 first = own[k, xx, core, us[2], :, lane_of(z)]
                 bz[k, xx] = (first + r1z[0, k, xx]) + (r1z[1, k, xx] + r1z[2, k, xx])
 
@@ -429,7 +427,8 @@
 
     gp_ref, g5_ref, g3_ref = (waves[i][0] for i in range(3))
     gp_ref[...] = tn(pooled_ref[...], upstream).reshape(gp_ref.shape)
-    move_p = reduce_wave(0, outp_ref)
+    move_p, move_5, move_3 = (reduce_wave(i, ref) for i, ref in enumerate((outp_ref, out5_ref, out3_ref)))
+    next(move_p)
     next(move_p)
     grad_pooled = nt(upstream, proj_ref[...]) * (0.5 / length)
 
@@ -454,25 +453,19 @@
     spread_back(channels)
     next(move_p)
     weigh(g5_ref, lambda: taps[...], channels)
+    next(move_5)
     weigh(g5_ref, lambda: taps[...], channels + 256)
-    move_5 = reduce_wave(1, out5_ref)
     next(move_5)
-    next(move_p)
     spread_back(0)
     next(move_5)
     weigh(g3_ref, lambda: taps[:, emb : 4 * emb], 0)
-    next(move_p)
+    next(move_3)
     weigh(g3_ref, lambda: taps[:, emb : 4 * emb], 256)
-    move_3 = reduce_wave(2, out3_ref)
     next(move_3)
     next(move_p)
-    next(move_5)
     next(move_3)
-    next(move_5)
-    next(move_3)
-    next(move_5)
-    next(move_3)
-    next(move_3)
+    for move in (move_p, move_5, move_3, move_p, move_5, move_3, move_5, move_3):
+        next(move)
     for move in (move_p, move_5, move_3):
         next(move)
     for copy in started + sent:
@@ -551,8 +544,8 @@
             dma((3, 9)),
             dma((2, 12)),
             dma((2, 12)),
-            dma((3,)),
-            dma((3,)),
+            dma((3, 2)),
+            dma((3, 2)),
             dma((9, 9)),
             dma((9, 9)),
             dma((3, 7)),
@@ -593,7 +586,8 @@
     free_vectors,
 ):
     tokens = jnp.concatenate([query_tokens.T.reshape(-1), label_tokens.T.reshape(-1)])
-    embedded = jnp.take(table, tokens, axis=0, mode="clip")
+    tokens = lax.optimization_barrier(tokens)
+    embedded = table.at[tokens].get(mode="promise_in_bounds")
     return training_window(
         embedded,
         three,

time: 117 us -> 112 us (0.957)
  Pallas kernels: 93.7 us -> 89 us
    pallas_call x1, Pallas kernels: 91.9 us -> 87.2 us  [training_window(): pl.pallas_call(window_kernel, out_shape=shapes, in_specs=[vmem, hbm, hbm,...]
where the time goes in v4:
time: 112 us
  Pallas kernels  89 us (79%)
  local copies, waits for them, and re-layouts  21.9 us (20%)
    pallas_call x1, Pallas kernels, training_window(): pl.pallas_call(window_kernel, out_shape=shapes, in_specs=[vmem, hbm, hbm,...  87.2 us
    gather x1, local copies, waits for them, and re-layouts, per_device(): embedded = table.at[tokens].get(mode='promise_in_bounds')  20.3 us

profile of v4, /device:TPU:1, one launch (start us, length us, event | category | flops | bytes accessed | tf_op | source)
XLA Modules:
  0.0 111.6 jit_solution(4762394960936378026)
XLA Ops:
  0.6 0.8 reshape.35
  1.4 0.8 copy.16
  2.2 0.1 reshape.34
  2.3 20.3 %gather_fusion = bf16[3072,256]{1,0:T(8,128)(2,1)} fusion(bf16[32768,256]{1,0:T(8,128)(2,1)} %param.17, s32[3072]{0:T(1024)S(1)} %fusion), kind=kCustom, calls=%fused_computation | custom fusion | bytes 3158016 | tf_op jit(solution)/shard_map/gather | solution.py:590
  22.6 87.2 %training_window.1 = (f32[1,32]{1,0:T(1,128)}, f32[16,512]{1,0:T(8,128)}, f32[2,3,8,512]{3,2,1,0:T(8,128)}, f32[2,5,8,512]{3,2,1,0:T(8,128)}, f32[2,4,8,512]{3,2,1,0:T(8,128)}) custom-call(bf16[3072,256]{1,0:T(8,128)(2,1)} %gather_fusion, bf16[768,512]{1,0:T(8,128)(2,1)} %w3_hbm.1, bf16[1280,512]{1,0:T(8,128)(2,1)} %w5_hbm.1, bf16[1024,512]{1,0:T(8,128)(2,1)} %proj_hbm.1, ...), custom_call_target="tpu_custom_call" | custom-call | tf_op jit(solution)/shard_map/training_window/pallas_call | solution.py:519
  109.8 1.8 %copy_out.1 = (f32[1,32]{1,0:T(1,128)}, f32[16,512]{1,0:T(8,128)}, f32[2,3,8,512]{3,2,1,0:T(8,128)}, f32[2,5,8,512]{3,2,1,0:T(8,128)}, f32[2,4,8,512]{3,2,1,0:T(8,128)}) custom-call(f32[1,32]{1,0:T(1,128)} %get-tuple-element.15.refs_0_, f32[16,512]{1,0:T(8,128)} %get-tuple-element.16.refs_1_, f32[2,3,8,512]{3,2,1,0:T(8,128)} %get-tuple-element.17.refs_2_, ...), custom_call_target="tpu_custom_call" | custom-call | tf_op jit(solution)/shard_map/copy_out/pallas_call | solution.py:559
  (2 shorter events, 0.0 us)

commit v5 on v4

--- a/solution.py
+++ b/solution.py
@@ -266,7 +266,7 @@
     loss_acc[...] = jnp.zeros_like(loss_acc)
     node = lax.broadcasted_iota(jnp.int32, (nodes, 512), 0).astype(f32) + 1.0
 
-    @pl.loop(0, 8, unroll=4)
+    @pl.loop(0, 8, unroll=8)
     def _(i):
         chunk = all_q[i // 2, i % 2].reshape(512, wide)
         keys = chunk[:, :width]
@@ -293,7 +293,7 @@
 
     own_rows = all_q[(*home, slice(None), pl.ds(0, width))]
 
-    @pl.loop(0, 8, unroll=4)
+    @pl.loop(0, 8, unroll=8)
     def _(i):
         keys = all_h[i // 2, i % 2].reshape(256, width)
         scores = SCORE_SCALE * nt(own_rows, keys)
@@ -438,7 +438,7 @@
             mine = grad_pooled[:queries] if titles == queries else grad_pooled[queries:]
             mine = mine[:, low : low + channels]
 
-            @pl.loop(0, length)
+            @pl.loop(0, length, unroll=4)
             def _(p):
                 span = pl.ds(pl.multiple_of(base + p * titles, 32), titles)
                 grad_pre[span, low : low + channels] = (

time: 112 us -> 111 us (level)
  no operation moved by 1% of the time
where the time goes in v5:
time: 111 us
  Pallas kernels  88.5 us (80%)
  local copies, waits for them, and re-layouts  21.7 us (20%)
    pallas_call x1, Pallas kernels, training_window(): pl.pallas_call(window_kernel, out_shape=shapes, in_specs=[vmem, hbm, hbm,...  86.7 us
    gather x1, local copies, waits for them, and re-layouts, per_device(): embedded = table.at[tokens].get(mode='promise_in_bounds')  20.1 us

profile of v5, /device:TPU:1, one launch (start us, length us, event | category | flops | bytes accessed | tf_op | source)
XLA Modules:
  0.0 110.9 jit_solution(13594603384749767156)
XLA Ops:
  0.6 0.8 reshape.35
  1.4 0.8 copy.16
  2.2 0.1 reshape.34
  2.3 20.1 %gather_fusion = bf16[3072,256]{1,0:T(8,128)(2,1)} fusion(bf16[32768,256]{1,0:T(8,128)(2,1)} %param.17, s32[3072]{0:T(1024)S(1)} %fusion), kind=kCustom, calls=%fused_computation | custom fusion | bytes 3158016 | tf_op jit(solution)/shard_map/gather | solution.py:590
  22.4 86.7 %training_window.1 = (f32[1,32]{1,0:T(1,128)}, f32[16,512]{1,0:T(8,128)}, f32[2,3,8,512]{3,2,1,0:T(8,128)}, f32[2,5,8,512]{3,2,1,0:T(8,128)}, f32[2,4,8,512]{3,2,1,0:T(8,128)}) custom-call(bf16[3072,256]{1,0:T(8,128)(2,1)} %gather_fusion, bf16[768,512]{1,0:T(8,128)(2,1)} %w3_hbm.1, bf16[1280,512]{1,0:T(8,128)(2,1)} %w5_hbm.1, bf16[1024,512]{1,0:T(8,128)(2,1)} %proj_hbm.1, ...), custom_call_target="tpu_custom_call" | custom-call | tf_op jit(solution)/shard_map/training_window/pallas_call | solution.py:519
  109.1 1.8 %copy_out.1 = (f32[1,32]{1,0:T(1,128)}, f32[16,512]{1,0:T(8,128)}, f32[2,3,8,512]{3,2,1,0:T(8,128)}, f32[2,5,8,512]{3,2,1,0:T(8,128)}, f32[2,4,8,512]{3,2,1,0:T(8,128)}) custom-call(f32[1,32]{1,0:T(1,128)} %get-tuple-element.15.refs_0_, f32[16,512]{1,0:T(8,128)} %get-tuple-element.16.refs_1_, f32[2,3,8,512]{3,2,1,0:T(8,128)} %get-tuple-element.17.refs_2_, ...), custom_call_target="tpu_custom_call" | custom-call | tf_op jit(solution)/shard_map/copy_out/pallas_call | solution.py:559
  (2 shorter events, 0.0 us)
